TPU v7x, 256 devices: a whole 4x4x8 slice. The times are simulated.
256 devices in a mesh: batch: 2 (over core), ctx: 32 (over z, x), head: 4 (over y).
Axes of the slice: x: 4, y: 4, z: 8, core: 2. Of those that a mesh axis runs over, the one named last changes fastest.
Arguments:
- queries: bfloat16 [32768, 2048], P(('batch', 'ctx'), 'head'), parts along dimension 0, may hold values from -6 to 6
- key_value: bfloat16 [32768, 2, 2048], P(('batch', 'ctx'), None, 'head'), parts along dimension 0, may hold values from -6 to 6
- out_weight: bfloat16 [2048, 4096], P('head'), may hold values from -2 to 2
- random_blocks: int32 [512, 3], P('batch'), parts along dimension 0, may hold values from 0 to 255, as said below
- global_ids: int32 [4], P('batch'), parts along dimension 0, may hold values from 0 to 255, as said below
Outputs:
- projected: bfloat16 [32768, 4096], P(('batch', 'ctx'), 'head'), parts along dimension 0
There are 2 independent parts, one for each index of `batch`. A program takes and returns all parts, laid end to end along the dimension named above; an argument that names none is the same for every part. Nothing has to cross between parts.
Inputs may be any that keep to these rules, and one draw needn't show every extreme that they name: `random_blocks`: row i lists random key blocks of query block i; entries may repeat. Among the 3 * 8 entries of the 8 aligned rows of one index of ctx, at most 2 lie in the blocks of any one index of ctx (blocks d * 8 to d * 8 + 7). In every draw there is one index of ctx, the same for all rows, whose blocks are named exactly 2 times by the rows of every index of ctx. `global_ids`: 2 distinct blocks; one of them is always the last block, 255, at a position drawn from the seed.
All inputs are finite; a program needn't handle non-finite values.
Results may differ from a plain program's by a relative error of at most 0.015.
Values may be sent and summed in bfloat16 or wider, within the bound.
No kernel may reach another device: no remote copies, remote signals or barrier semaphores. Data moves between devices by JAX's collectives and lax.ppermute only.
A program may use at most 128 MiB of HBM per device.

v0:
```python
import math

import jax
import jax.numpy as jnp
from jax import lax
from jax.sharding import PartitionSpec as P

DH = 128
BLK = 64


def padded(block, sides, width):
    for axis, dim in sides:
        count = lax.axis_size(axis)
        forward = [(i, i + 1) for i in range(count - 1)]
        backward = [(target, source) for source, target in forward]
        low = lax.ppermute(
            lax.slice_in_dim(block, block.shape[dim] - width, None, axis=dim), axis, forward
        )
        high = lax.ppermute(lax.slice_in_dim(block, 0, width, axis=dim), axis, backward)
        block = jnp.concatenate([low, block, high], axis=dim)
    return block


def combined_all(value, axis, combine):
    everything = jax.tree.map(lambda part: lax.all_gather(part, axis), value)
    leading = jax.tree.map(lambda part: part[0], everything)

    def lap(k, so_far):
        return combine(so_far, jax.tree.map(lambda part: part[k], everything))

    return lax.fori_loop(1, lax.axis_size(axis), lap, leading)


def combine_rows(earlier_part, later_part):
    max_early, tot_early, acc_early = earlier_part
    max_later, tot_later, acc_later = later_part
    joint = jnp.maximum(max_early, max_later)
    factor_early = jnp.exp(max_early - joint)
    factor_later = jnp.exp(max_later - joint)
    softmax_totals = tot_early * factor_early + tot_later * factor_later
    summed = acc_early * factor_early[..., None] + acc_later * factor_later[..., None]
    return (joint, softmax_totals, summed)


def body(queries, key_value, out_weight, random_blocks, global_ids):
    ctx_count = lax.axis_size("ctx")
    position = lax.axis_index("ctx")
    tokens = queries.shape[0]
    width_here = queries.shape[1]
    heads_here = width_here // DH
    blocks_here = tokens // BLK
    total_blocks = blocks_here * ctx_count
    picks = random_blocks.shape[1]
    glob_count = global_ids.shape[0]
    capacity = max(2, (picks * blocks_here + ctx_count - 1) // ctx_count)
    score_scaling = 1.0 / math.sqrt(DH)
    query_blocks = queries.reshape(blocks_here, BLK, heads_here, DH)
    kv_blocks = key_value.reshape(blocks_here, BLK, 2, width_here)
    extended = padded(key_value, (("ctx", 0),), BLK)
    ext_blocks = extended.reshape(blocks_here + 2, BLK, 2, width_here)
    window = jnp.stack([ext_blocks[:-2], ext_blocks[1:-1], ext_blocks[2:]], axis=1)
    global_owner = global_ids // blocks_here
    global_local = global_ids - global_owner * blocks_here
    owned = global_owner == position
    glob_query = jnp.where(
        owned[:, None, None],
        queries.reshape(blocks_here, BLK, width_here)[global_local].astype(jnp.float32),
        0.0,
    )
    glob_kv = jnp.where(
        owned[:, None, None, None], kv_blocks[global_local].astype(jnp.float32), 0.0
    )
    glob_query, glob_kv = (
        lax.psum(glob_query.astype(jnp.bfloat16), "ctx").astype(jnp.float32),
        lax.psum(glob_kv.astype(jnp.bfloat16), "ctx").astype(jnp.float32),
    )
    glob_query = glob_query.astype(jnp.bfloat16)
    glob_kv = glob_kv.astype(jnp.bfloat16)
    slot_count = picks * blocks_here
    block_ids = random_blocks.reshape(ctx_count, slot_count)
    owners = block_ids // blocks_here
    local_index = block_ids - owners * blocks_here
    slot_range = jnp.arange(slot_count, dtype=jnp.int32)
    earlier = slot_range[None, :] < slot_range[:, None]
    same_owner = owners[:, :, None] == owners[:, None, :]
    slot_rank = jnp.sum(same_owner & earlier[None], axis=2)
    to_here = owners == position
    matches = to_here[:, :, None] & (
        slot_rank[:, :, None] == jnp.arange(capacity, dtype=jnp.int32)[None, None, :]
    )
    chosen = jnp.sum(jnp.where(matches, local_index[:, :, None], 0), axis=1)
    outgoing = kv_blocks[chosen]
    incoming = lax.all_to_all(outgoing, "ctx", split_axis=0, concat_axis=0, tiled=True)
    my_owners = lax.dynamic_index_in_dim(owners, position, 0, keepdims=False)
    my_rank = lax.dynamic_index_in_dim(slot_rank, position, 0, keepdims=False)
    fetched = incoming.reshape(ctx_count * capacity, BLK, 2, width_here)[
        my_owners * capacity + my_rank
    ]
    fetched = fetched.reshape(blocks_here, picks, BLK, 2, width_here)
    glob_part = jnp.broadcast_to(glob_kv[None], (blocks_here,) + glob_kv.shape)
    listed = jnp.concatenate([window, glob_part, fetched], axis=1)
    listed_count = listed.shape[1]
    gathered_key_rows = listed[:, :, :, 0].reshape(blocks_here, listed_count * BLK, heads_here, DH)
    gathered_value_rows = listed[:, :, :, 1].reshape(
        blocks_here, listed_count * BLK, heads_here, DH
    )
    block_number = position * blocks_here + jnp.arange(blocks_here, dtype=jnp.int32)
    usable = jnp.concatenate(
        [
            (block_number > 0)[:, None],
            jnp.ones((blocks_here, 1), bool),
            (block_number < total_blocks - 1)[:, None],
            jnp.ones((blocks_here, listed_count - 3), bool),
        ],
        axis=1,
    )
    key_mask = jnp.repeat(usable, BLK, axis=1)
    logit_scores = (
        jnp.einsum(
            "bqhd,bkhd->bhqk", query_blocks, gathered_key_rows, preferred_element_type=jnp.float32
        )
        * score_scaling
    )
    logit_scores = jnp.where(key_mask[:, None, None, :], logit_scores, -jnp.inf)
    row_max = jnp.max(logit_scores, axis=-1, keepdims=True)
    weights = jnp.exp(logit_scores - row_max)
    softmax_totals = jnp.sum(weights, axis=-1)
    attended_values = jnp.einsum(
        "bhqk,bkhd->bqhd",
        weights.astype(jnp.bfloat16),
        gathered_value_rows,
        preferred_element_type=jnp.float32,
    )
    attended_values = attended_values / jnp.transpose(softmax_totals, (0, 2, 1))[..., None]
    glob_heads = glob_query.reshape(glob_count, BLK, heads_here, DH)
    local_keys = key_value[:, 0].reshape(tokens, heads_here, DH)
    local_values = key_value[:, 1].reshape(tokens, heads_here, DH).astype(jnp.float32)
    glob_scores = (
        jnp.einsum("gqhd,khd->ghqk", glob_heads, local_keys, preferred_element_type=jnp.float32)
        * score_scaling
    )
    glob_max = jnp.max(glob_scores, axis=-1)
    glob_weights = jnp.exp(glob_scores - glob_max[..., None])
    glob_totals = jnp.sum(glob_weights, axis=-1)
    glob_acc = jnp.einsum(
        "ghqk,khd->ghqd", glob_weights, local_values, precision=lax.Precision.HIGHEST
    )
    glob_max, glob_totals, glob_acc = combined_all(
        (glob_max, glob_totals, glob_acc), "ctx", combine_rows
    )
    glob_out = jnp.transpose(glob_acc / glob_totals[..., None], (0, 2, 1, 3))
    here_block = jnp.arange(blocks_here, dtype=jnp.int32)
    is_global = owned[None, :] & (global_local[None, :] == here_block[:, None])
    any_global = jnp.any(is_global, axis=1)
    which_global = jnp.sum(
        jnp.where(is_global, jnp.arange(glob_count, dtype=jnp.int32)[None, :], 0), axis=1
    )
    attended_values = jnp.where(
        any_global[:, None, None, None], glob_out[which_global], attended_values
    )
    attention = attended_values.astype(jnp.bfloat16).reshape(tokens, width_here)
    partial_terms = jnp.dot(attention, out_weight, preferred_element_type=jnp.float32)
    summed = lax.psum_scatter(
        partial_terms.astype(jnp.bfloat16), "head", scatter_dimension=1, tiled=True
    )
    return summed


def solution(mesh):
    in_specs = (
        P(("batch", "ctx"), "head"),
        P(("batch", "ctx"), None, "head"),
        P("head", None),
        P("batch", None),
        P("batch"),
    )
    out_specs = P(("batch", "ctx"), "head")
    return jax.shard_map(body, mesh=mesh, in_specs=in_specs, out_specs=out_specs, check_vma=False)
```

profile of v0, /device:TPU:103, one launch (start us, length us, event | category | flops | bytes accessed | tf_op | source)
XLA Modules:
  0.0 527.8 jit_solution(9310758939520394296)
XLA Ops:
  9.3 19.6 %gather_fusion.3 = bf16[64,64,2,512]{3,2,1,0:T(2,128)(2,1)} fusion(bf16[8,64,2,512]{3,2,1,0:T(2,128)(2,1)} %bitcast.102, s32[1024]{0:T(1024)S(1)} %get-tuple-element.264), kind=kCustom, calls=%fused_computation.3 | custom fusion | bytes 16777472 | tf_op jit(solution)/shard_map/gather | solution.py:93
  28.9 8.8 %copy.126 = bf16[64,64,2,512]{3,1,2,0:T(8,128)(2,1)} copy(bf16[64,64,2,512]{3,2,1,0:T(2,128)(2,1)} %gather_fusion.3) | data formatting | bytes 16777216 | tf_op jit(solution)/shard_map/gather | solution.py:93
  37.8 9.8 %all-to-all-start = ((bf16[32,2,64,2,512]{4,2,3,1,0:T(8,128)(2,1)}), bf16[32,2,64,2,512]{4,2,3,1,0:T(8,128)(2,1)}, u32[]{:S(2)}, u32[]{:S(2)}) async-start(bf16[32,2,64,2,512]{4,2,3,1,0:T(8,128)(2,1)} %bitcast.105), calls=%async_computation | async-start | bytes 16777216 | tf_op jit(solution)/shard_map/all_to_all | solution.py:94
  48.8 1.6 gather_fusion
  52.1 1.5 fusion.45
  53.7 2.3 copy.144
  55.9 1.3 copy.145
  57.3 215.5 %all-reduce.3.cloned.1.call-done = (bf16[2,64,4,128]{3,1,0,2:T(8,128)(2,1)}, bf16[2,64,2,512]{3,2,1,0:T(2,128)(2,1)}) async-done(((bf16[2,64,4,128]{3,1,0,2:T(8,128)(2,1)}, bf16[2,64,2,512]{3,2,1,0:T(2,128)(2,1)}), (bf16[2,64,4,128]{3,1,0,2:T(8,128)(2,1)}, bf16[2,64,2,512]{3,2,1,0:T(2,128)(2,1)})) %all-reduce.3.cloned.1.call-update) | async-done | bytes 393232 | tf_op jit(solution)/shard_map/psum | solution.py:75
  272.8 1.5 fusion.46
  274.3 1.5 convolution_bitcast_fusion
  276.0 4.3 collective-permute-start
  280.3 1.9 collective-permute-start.1
  284.2 5.1 collective-permute-done.1
  289.3 2.7 pad_maximum_fusion
  295.9 33.3 %all-gather.1 = f32[64,4,64]{2,1,0:T(4,128)S(1)} all-gather(f32[2,4,64]{2,1,0:T(4,128)S(1)} %copy.113), channel_id=3, replica_groups=mesh['batch'=2,'ctx'=32,'head'=4] {'ctx'}, dimensions={0}, use_global_device_ids=true | all-gather | bytes 67584 | tf_op jit(solution)/shard_map/all_gather | solution.py:26
  329.2 37.8 %all-gather = f32[64,4,64]{2,1,0:T(4,128)S(1)} all-gather(f32[2,4,64]{2,1,0:T(4,128)S(1)} %copy.112), channel_id=2, replica_groups=mesh['batch'=2,'ctx'=32,'head'=4] {'ctx'}, dimensions={0}, use_global_device_ids=true | all-gather | bytes 67584 | tf_op jit(solution)/shard_map/all_gather | solution.py:26
  367.0 1.6 broadcast_dynamic-update-slice_fusion
  368.5 4.2 gather_fusion.4
  372.7 1.9 copy_dynamic-update-slice_fusion
  374.6 5.9 %fusion.43 = (bf16[8,8,64,1,512]{4,2,1,0,3:T(8,128)(2,1)}, bf16[8,8,64,1,512]{4,2,1,0,3:T(8,128)(2,1)}) fusion(bf16[8,8,64,2,512]{4,2,1,0,3:T(8,128)(2,1)} %copy_dynamic-update-slice_fusion), kind=kLoop, calls=%fused_computation.93 | loop fusion | bytes 16777216 | tf_op jit(solution)/shard_map/slice | solution.py:104
  380.6 6.9 %reshape_squeeze.15 = bf16[8,512,4,128]{3,2,1,0:T(4,128)(2,1)} reshape(bf16[8,8,64,1,512]{4,2,1,0,3:T(8,128)(2,1)} %get-tuple-element.250) | data formatting | bytes 8388608 | tf_op jit(solution)/shard_map/reshape;squeeze | solution.py:104
  387.5 7.0 %reshape_squeeze.14 = bf16[8,512,4,128]{3,2,1,0:T(4,128)(2,1)} reshape(bf16[8,8,64,1,512]{4,2,1,0,3:T(8,128)(2,1)} %get-tuple-element.251) | data formatting | bytes 8388608 | tf_op jit(solution)/shard_map/reshape;squeeze | solution.py:105
  394.4 3.9 bitcast_reduce_fusion
  398.3 1.9 copy-done.1
  400.3 1.5 fusion.9
  402.8 39.3 %while.19 = (s32[]{:T(128)}, f32[2,4,64]{2,1,0:T(4,128)S(1)}, f32[2,4,64]{2,1,0:T(4,128)S(1)}, f32[2,4,64,128]{3,2,1,0:T(8,128)S(1)}, f32[32,2,4,64]{3,2,1,0:T(4...) while((s32[]{:T(128)}, f32[2,4,64]{2,1,0:T(4,128)S(1)}, ...), condition=%wide.region_5.6_spmd, body=%wide.region_4.5_spmd.sunk | while | flops 199685 | bytes 807063 | solution.py:32
  410.4 1.2 fusion.55
  420.6 1.2 fusion.55
  434.6 1.2 fusion.55
  442.9 5.3 %select_convert_fusion = bf16[8,64,4,128]{3,1,2,0:T(8,128)(2,1)S(1)} fusion(bf16[8,64,4,128]{3,1,2,0:T(8,128)(2,1)S(1)} %gather_fusion.1, bf16[8,512,4,128]{3,2,1,0:T(4,128)(2,1)} %reshape_squeeze.14, f32[8,4,512,64]{2,3,1,0:T(8,128)} %copy-done.1, f32[8,4,64]{2,1,0:T(4,128)S(1)} %get-tuple-element.262, pred[8,512]{1,0:T(8,128)(4,1)S(1)} %broadcast_in_dim.130, ...), kind=kOutput, calls=%fused_computation.40 | convolution fusion | flops 273154048 | bytes 9457672 | tf_op jit(solution)/shard_map/bhqk,bkhd->bqhd/dot_general | solution.py:129
  448.7 4.3 convolution_convert_fusion
  453.0 68.2 %reduce-scatter.2.cloned.1.call-done = bf16[512,1024]{1,0:T(8,128)(2,1)} async-done(((bf16[512,4096]{1,0:T(8,128)(2,1)}), bf16[512,1024]{1,0:T(8,128)(2,1)}) %reduce-scatter.2.cloned.1.call-update) | async-done | bytes 1048592 | tf_op jit(solution)/shard_map/reduce_scatter | solution.py:164
  (128 shorter events, 48.8 us)
Async XLA Ops:
  37.8 9.9 %copy-start = (bf16[512,2,512]{2,1,0:T(2,128)(2,1)S(1)}, bf16[512,2,512]{2,1,0:T(2,128)(2,1)}, u32[]{:S(2)}) copy-start(bf16[512,2,512]{2,1,0:T(2,128)(2,1)} %param.8) | copy-start | bytes 3145732
  37.8 330.7 %all-to-all-start = ((bf16[32,2,64,2,512]{4,2,3,1,0:T(8,128)(2,1)}), bf16[32,2,64,2,512]{4,2,3,1,0:T(8,128)(2,1)}, u32[]{:S(2)}, u32[]{:S(2)}) async-start(bf16[32,2,64,2,512]{4,2,3,1,0:T(8,128)(2,1)} %bitcast.105), calls=%async_computation | async-start | bytes 16777216 | tf_op jit(solution)/shard_map/all_to_all | solution.py:94
  47.6 225.1 %all-reduce.3.cloned.1.call-start = ((), (), s32[]{:S(2)}) async-start(), calls=%async_computation.4 | async-start | bytes 786432 | tf_op jit(solution)/shard_map/psum | solution.py:75
  52.1 349.7 %all-gather.5.cloned.1.call-start = ((), (), s32[]{:S(2)}) async-start(), calls=%async_computation.3 | async-start | bytes 8650752 | tf_op jit(solution)/shard_map/all_gather | solution.py:26
  55.9 227.0 %copy-start.2 = (bf16[512,512]{1,0:T(8,128)(2,1)S(1)}, bf16[512,512]{1,0:T(8,128)(2,1)}, u32[]{:S(2)}) copy-start(bf16[512,512]{1,0:T(8,128)(2,1)} %param.7) | copy-start | bytes 1572868
  275.7 245.5 %reduce-scatter.2.cloned.1.call-start = ((), (), s32[]{:S(2)}) async-start(), calls=%async_computation.2 | async-start | bytes 5242880 | tf_op jit(solution)/shard_map/reduce_scatter | solution.py:164
  276.0 8.2 %collective-permute-start = (bf16[64,2,512]{2,1,0:T(2,128)(2,1)S(1)}, bf16[64,2,512]{2,1,0:T(2,128)(2,1)S(1)}, u32[]{:S(2)}, u32[]{:S(2)}) collective-permute-start(bf16[64,2,512]{2,1,0:T(2,128)(2,1)S(1)} %get-tuple-element.255), channel_id=1, source_target_pairs={{0,4},{4,8},{8,12},{12,16},{16,20},{20,24},{24,28},{28,32},{32,36}... | collective-permute-start | bytes 393224 | tf_op jit(solution)/shard_map/ppermute | solution.py:17
  280.3 9.0 %collective-permute-start.1 = (bf16[64,2,512]{2,1,0:T(2,128)(2,1)S(1)}, bf16[64,2,512]{2,1,0:T(2,128)(2,1)S(1)}, u32[]{:S(2)}, u32[]{:S(2)}) collective-permute-start(bf16[64,2,512]{2,1,0:T(2,128)(2,1)S(1)} %get-tuple-element.254), channel_id=1, source_target_pairs={{4,0},{8,4},{12,8},{16,12},{20,16},{24,20},{28,24},{32,28},{36,32}... | collective-permute-start | bytes 393224 | tf_op jit(solution)/shard_map/ppermute | solution.py:20
  284.1 11.4 %copy-start.4 = (bf16[2,64,2,512]{3,2,1,0:T(2,128)(2,1)S(1)}, bf16[2,64,2,512]{3,2,1,0:T(2,128)(2,1)}, u32[]{:S(2)}) copy-start(bf16[2,64,2,512]{3,2,1,0:T(2,128)(2,1)} %get-tuple-element.241) | copy-start | bytes 786436
  387.5 7.0 %copy-start.3 = (bf16[8,64,4,128]{3,2,1,0:T(4,128)(2,1)S(1)}, bf16[8,64,4,128]{3,2,1,0:T(4,128)(2,1)}, u32[]{:S(2)}) copy-start(bf16[8,64,4,128]{3,2,1,0:T(4,128)(2,1)} %reshape.215) | copy-start | bytes 1572868
  398.3 1.9 copy-start.1
  442.9 5.7 %copy-start.5 = (bf16[512,4096]{1,0:T(8,128)(2,1)S(1)}, bf16[512,4096]{1,0:T(8,128)(2,1)}, u32[]{:S(2)}) copy-start(bf16[512,4096]{1,0:T(8,128)(2,1)} %param.9) | copy-start | bytes 12582916
Sparse Core Ops, SparseCore 0:
  52.2 220.5 all-reduce.2
  275.9 101.1 all-gather.4
  453.1 68.0 reduce-scatter.1
where the time goes:
time: 526 us; the launch traced here: 528 us
  waiting for transfers between devices  289 us (55%)
  local copies, waits for them, and re-layouts  74 us (14%)
  blocking collectives  71 us (13%)
  other arithmetic  47 us (9%)
  matrix products  16.4 us (3%)
  starting transfers between devices  16.2 us (3%)
  between operations  13.4 us (3%)
    psum x1, waiting for transfers between devices, body(): lax.psum(glob_query.astype(jnp.bfloat16), 'ctx').astype(jnp.float32)  216 us
    all_gather x2, blocking collectives, combined_all(): everything = jax.tree.map(lambda part: lax.all_gather(part, axis), value)  71 us
    reduce_scatter x1, waiting for transfers between devices, body(): lax.psum_scatter(partial_terms.astype(jnp.bfloat16), 'head', scatter_dime...  68.2 us
    add x31, other arithmetic, combine_rows(): acc_early * factor_early[..., None] + acc_later * factor_later[..., None]  37.7 us
    gather x2, local copies, waits for them, and re-layouts, body(): outgoing = kv_blocks[chosen]  28.5 us
    unnamed x19, local copies, waits for them, and re-layouts  11.4 us
  transfers between devices with their start and end apart: 6, of which 3 were waited for; matrix products, arithmetic and copies ran while one was open for 10% of the time, Pallas kernels for 0%

commit v1 on v0

v1 whole, which is shorter than its diff:
```python
import functools
import math

import jax
import jax.numpy as jnp
from jax import lax
from jax.experimental import pallas as pl
from jax.experimental.pallas import tpu as pltpu
from jax.sharding import Mesh
from jax.sharding import PartitionSpec as P

DH = 128
BLK = 64
NEG = -1e30
NZ = 8
NX = 4
NY = 4
BPD = 8
TOK = BLK * BPD
PAIR = 2
WIDE = PAIR * DH
STAT = 16
GROUP = 4
QBS = NX * BPD
SCALE = 1.0 / math.sqrt(DH)
VMEM = 48 * 1024 * 1024

any_space = pl.BlockSpec(memory_space=pl.ANY)
in_vmem = pl.BlockSpec(memory_space=pltpu.VMEM)
in_smem = pl.BlockSpec(memory_space=pltpu.SMEM)


def shift(count, by):
    return [(i, (i + by) % count) for i in range(count)]


def lists_kernel(table, glob, place, count, index, dense):
    z, x = place[0], place[1]
    for k in range(QBS * 8 + 8):
        index[k] = 0
    for g in range(2):
        owner = glob[g] >> 3
        slot = (x - (owner & 3)) & 3
        dense[g] = jnp.where((owner >> 2) == z, slot * BPD + (glob[g] & 7), -1)

    def one(qb, carry):
        qx = (x - (qb >> 3)) & 3
        block = ((z * NX + qx) << 3) + (qb & 7)
        entries = [(block - 1, block > 0), (block, None)]
        entries += [(block + 1, block < NZ * NX * BPD - 1)]
        entries += [(glob[0], None), (glob[1], None)]
        entries += [(table[block * 3 + j], None) for j in range(3)]
        filled = jnp.int32(0)
        for key, exists in entries:
            key = jnp.clip(key, 0, NZ * NX * BPD - 1)
            owner = key >> 3
            here = (owner & 3) == x
            if exists is not None:
                here = here & exists
            index[qb * 8 + filled] = ((((owner >> 2) - z) & 7) << 3) + (key & 7)
            filled = filled + here.astype(jnp.int32)
        is_global = (block == glob[0]) | (block == glob[1])
        count[qb] = jnp.where(is_global, 0, filled)
        return carry

    lax.fori_loop(0, QBS, one, 0)


def make_lists(table, glob, place):
    return pl.pallas_call(
        lists_kernel,
        out_shape=[
            jax.ShapeDtypeStruct((QBS,), jnp.int32),
            jax.ShapeDtypeStruct((QBS * 8 + 8,), jnp.int32),
            jax.ShapeDtypeStruct((2,), jnp.int32),
        ],
        in_specs=[in_smem] * 3,
        out_specs=[in_smem] * 3,
    )(table, glob, place)


def dot_t(a, b):
    return lax.dot_general(a, b, (((1,), (1,)), ((), ())), preferred_element_type=jnp.float32)


def attend_kernel(chunk, *refs):
    count, index, dense = refs[:3]
    q_in = refs[3:7]
    kv_in = refs[7:14]
    k_far, v_far = refs[14:16]
    out = refs[16:20]
    q_s, kv_s, o_s, stat, sems = refs[20:]
    copies = []
    for s in range(NX):
        copies.append((q_in[s].at[:, pl.ds(chunk * WIDE, WIDE)], q_s.at[s]))
    for p in range(7):
        copies.append((kv_in[p], kv_s.at[p if p < 4 else p + 1]))
    copies.append((k_far, kv_s.at[4, 0]))
    copies.append((v_far, kv_s.at[4, 1]))
    copies = [pltpu.make_async_copy(a, b, sems.at[n]) for n, (a, b) in enumerate(copies)]
    for copy in copies:
        copy.start()
    for copy in copies:
        copy.wait()

    def finish(slot, local, head, m, total, acc):
        safe = jnp.maximum(total, 1e-30)
        rows = pl.ds(pl.multiple_of(local * BLK, BLK), BLK)
        o_s[slot, rows, head * DH : (head + 1) * DH] = (acc / safe).astype(jnp.bfloat16)
        lse = jnp.where(total > 0.0, m + jnp.log(safe), NEG)
        stat[head, pl.ds(pl.multiple_of((slot * BPD + local) * BLK, BLK), BLK), :] = (
            jnp.broadcast_to(lse, (BLK, DH))
        )

    def load_q(slot, local, head):
        rows = pl.ds(pl.multiple_of(local * BLK, BLK), BLK)
        return q_s[slot, rows, head * DH : (head + 1) * DH]

    lane = lax.broadcasted_iota(jnp.int32, (BLK, 2 * BLK), 1)

    def group(g, carry):
        counts = [count[g * GROUP + i] for i in range(GROUP)]
        most = functools.reduce(jnp.maximum, counts)
        slot = g // (BPD // GROUP)
        first = (g % (BPD // GROUP)) * GROUP
        chains = [(i, h) for i in range(GROUP) for h in range(PAIR)]

        def step(t, state):
            out_state = []
            for n, (i, h) in enumerate(chains):
                m, total, acc = state[n]
                base = (g * GROUP + i) * 8 + 2 * t
                cols = slice(h * DH, (h + 1) * DH)
                keys, values = [], []
                for e in range(2):
                    entry = index[base + e]
                    piece = entry >> 3
                    rows = pl.ds(pl.multiple_of((entry & 7) * BLK, BLK), BLK)
                    keys.append(kv_s[piece, 0, rows, cols])
                    values.append(kv_s[piece, 1, rows, cols])
                keys = jnp.concatenate(keys, axis=0)
                values = jnp.concatenate(values, axis=0)
                live = lane < (counts[i] - 2 * t) * BLK
                scores = dot_t(load_q(slot, first + i, h), keys) * SCALE
                scores = jnp.where(live, scores, NEG)
                m_new = jnp.maximum(m, jnp.max(scores, axis=1, keepdims=True))
                weights = jnp.where(live, jnp.exp(scores - m_new), 0.0)
                keep = jnp.exp(m - m_new)
                total = total * keep + jnp.sum(weights, axis=1, keepdims=True)
                acc = acc * keep + jnp.dot(
                    weights.astype(jnp.bfloat16), values, preferred_element_type=jnp.float32
                )
                out_state.append((m_new, total, acc))
            return tuple(out_state)

        start = tuple(
            (
                jnp.full((BLK, 1), NEG, jnp.float32),
                jnp.zeros((BLK, 1), jnp.float32),
                jnp.zeros((BLK, DH), jnp.float32),
            )
            for _ in chains
        )
        state = lax.fori_loop(0, (most + 1) // 2, step, start)
        for (i, h), (m, total, acc) in zip(chains, state):
            finish(slot, first + i, h, m, total, acc)
        return carry

    lax.fori_loop(0, QBS // GROUP, group, 0)

    for g in range(2):

        @pl.when(dense[g] >= 0)
        def _(g=g):
            slot = dense[g] >> 3
            local = dense[g] & 7

            def step(p, state):
                out_state = []
                for h in range(PAIR):
                    m, total, acc = state[h]
                    cols = slice(h * DH, (h + 1) * DH)
                    scores = dot_t(load_q(slot, local, h), kv_s[p, 0, :, cols]) * SCALE
                    m_new = jnp.maximum(m, jnp.max(scores, axis=1, keepdims=True))
                    weights = jnp.exp(scores - m_new)
                    keep = jnp.exp(m - m_new)
                    total = total * keep + jnp.sum(weights, axis=1, keepdims=True)
                    acc = acc * keep + jnp.dot(
                        weights.astype(jnp.bfloat16),
                        kv_s[p, 1, :, cols],
                        preferred_element_type=jnp.float32,
                    )
                    out_state.append((m_new, total, acc))
                return tuple(out_state)

            start = tuple(
                (
                    jnp.full((BLK, 1), NEG, jnp.float32),
                    jnp.zeros((BLK, 1), jnp.float32),
                    jnp.zeros((BLK, DH), jnp.float32),
                )
                for _ in range(PAIR)
            )
            state = lax.fori_loop(0, NZ, step, start)
            for h in range(PAIR):
                finish(slot, local, h, *state[h])

    eye = lax.broadcasted_iota(jnp.int32, (DH, DH), 0) == lax.broadcasted_iota(
        jnp.int32, (DH, DH), 1
    )
    for s in range(NX):
        for h in range(PAIR):
            lines = []
            for t in range(TOK // DH):
                tile = stat[h, s * TOK + t * DH : s * TOK + (t + 1) * DH, :]
                lines.append(jnp.sum(jnp.where(eye, tile, 0.0), axis=0, keepdims=True))
            left = jnp.concatenate(lines, axis=0)
            terms = []
            for _ in range(3):
                term = left.astype(jnp.bfloat16).astype(jnp.float32)
                terms.append(term)
                left = left - term
            terms.append(jnp.zeros_like(left))
            o_s[s, TOK : TOK + STAT, h * DH : (h + 1) * DH] = jnp.concatenate(
                terms, axis=0
            ).astype(jnp.bfloat16)
    back = [pltpu.make_async_copy(o_s.at[s], out[s], sems.at[s]) for s in range(NX)]
    for copy in back:
        copy.start()
    for copy in back:
        copy.wait()


def attend(chunk, lists, queries, pieces, k_far, v_far):
    message = jax.ShapeDtypeStruct((TOK + STAT, WIDE), jnp.bfloat16)
    return pl.pallas_call(
        functools.partial(attend_kernel, chunk),
        out_shape=[message] * NX,
        in_specs=[in_smem] * 3 + [any_space] * 13,
        out_specs=[any_space] * NX,
        scratch_shapes=[
            pltpu.VMEM((NX, TOK, WIDE), jnp.bfloat16),
            pltpu.VMEM((NZ, 2, TOK, WIDE), jnp.bfloat16),
            pltpu.VMEM((NX, TOK + STAT, WIDE), jnp.bfloat16),
            pltpu.VMEM((PAIR, NX * TOK, DH), jnp.float32),
            pltpu.SemaphoreType.DMA((13,)),
        ],
        compiler_params=pltpu.CompilerParams(vmem_limit_bytes=VMEM),
        cost_estimate=pl.CostEstimate(
            flops=1_500_000_000, bytes_accessed=8_000_000, transcendentals=2_000_000
        ),
    )(*lists, *queries, *pieces, k_far, v_far)


def join_kernel(m0, m1, m2, m3, out):
    shares = (m0, m1, m2, m3)
    eye = lax.broadcasted_iota(jnp.int32, (DH, DH), 0) == lax.broadcasted_iota(
        jnp.int32, (DH, DH), 1
    )
    for h in range(PAIR):
        cols = slice(h * DH, (h + 1) * DH)
        stats = []
        for share in shares:
            terms = share[TOK : TOK + STAT, cols].astype(jnp.float32)
            stats.append(terms[0:4] + terms[4:8] + terms[8:12])
        for t in range(TOK // DH):
            lse = [
                jnp.sum(
                    jnp.where(eye, jnp.broadcast_to(s[t : t + 1], (DH, DH)), 0.0),
                    axis=1,
                    keepdims=True,
                )
                for s in stats
            ]
            top = functools.reduce(jnp.maximum, lse)
            scale = [jnp.exp(v - top) for v in lse]
            norm = functools.reduce(jnp.add, scale)
            rows = slice(t * DH, (t + 1) * DH)
            terms = [f * s[rows, cols].astype(jnp.float32) for f, s in zip(scale, shares)]
            out[rows, cols] = (functools.reduce(jnp.add, terms) / norm).astype(jnp.bfloat16)


def join(messages):
    return pl.pallas_call(
        join_kernel,
        out_shape=jax.ShapeDtypeStruct((TOK, WIDE), jnp.bfloat16),
        in_specs=[in_vmem] * NX,
        out_specs=in_vmem,
        compiler_params=pltpu.CompilerParams(vmem_limit_bytes=VMEM),
        cost_estimate=pl.CostEstimate(
            flops=4_000_000, bytes_accessed=1_300_000, transcendentals=8_000
        ),
    )(*messages)


def project_kernel(last, *refs):
    att, weight = refs[:NY], refs[NY : 2 * NY]
    total = functools.reduce(
        jnp.add,
        [jnp.dot(a[...], w[...], preferred_element_type=jnp.float32) for a, w in zip(att, weight)],
    )
    if last:
        total = total + refs[2 * NY][...]
    refs[-1][...] = total.astype(refs[-1].dtype)


def project(chunk, att, weight, so_far=None):
    last = so_far is not None
    columns = weight[0].shape[1]
    tile = 256
    out_spec = pl.BlockSpec((TOK, tile), lambda j: (0, j))
    return pl.pallas_call(
        functools.partial(project_kernel, last),
        grid=(columns // tile,),
        out_shape=jax.ShapeDtypeStruct((TOK, columns), jnp.bfloat16 if last else jnp.float32),
        in_specs=[pl.BlockSpec((TOK, WIDE), lambda j: (0, 0))] * NY
        + [pl.BlockSpec((WIDE, tile), lambda j: (chunk, j))] * NY
        + [out_spec] * last,
        out_specs=out_spec,
        compiler_params=pltpu.CompilerParams(vmem_limit_bytes=VMEM),
        cost_estimate=pl.CostEstimate(
            flops=1_073_741_824, bytes_accessed=5_000_000, transcendentals=0
        ),
    )(*att, *weight, *([so_far] if last else []))


def ring_step(right, left):
    return (
        lax.ppermute(right, "z", shift(NZ, 1)),
        lax.ppermute(left, "z", shift(NZ, -1)),
    )


def body(queries, key_value, out_weight, random_blocks, global_ids):
    z, x, y = lax.axis_index("z"), lax.axis_index("x"), lax.axis_index("head")
    split = jnp.transpose(key_value, (1, 0, 2))
    own = [split[:, :, c * WIDE : (c + 1) * WIDE] for c in range(2)]
    place = jnp.stack([z, x]).astype(jnp.int32)
    lists = make_lists(random_blocks.reshape(-1), global_ids, place)
    behind = [[own[c]] for c in range(2)]
    ahead = [[own[c]] for c in range(2)]
    for _ in range(3):
        for c in range(2):
            right, left = ring_step(behind[c][-1], ahead[c][-1])
            behind[c].append(right)
            ahead[c].append(left)
    far = [ring_step(behind[c][3][0], ahead[c][3][1]) for c in range(2)]
    all_queries = [queries] + [lax.ppermute(queries, "x", shift(NX, s)) for s in range(1, NX)]
    columns = out_weight.shape[1] // NY
    weight = []
    for s in range(NY):
        part = lax.dynamic_slice_in_dim(out_weight, ((y + s) % NY) * columns, columns, axis=1)
        weight.append(part if s == 0 else lax.ppermute(part, "head", shift(NY, s)))
    total = None
    for c in range(2):
        pieces = ahead[c] + behind[c][:0:-1]
        messages = attend(c, lists, all_queries, pieces, *far[c])
        shares = [messages[0]] + [
            lax.ppermute(messages[s], "x", shift(NX, -s)) for s in range(1, NX)
        ]
        att = join(shares)
        everyone = [att] + [lax.ppermute(att, "head", shift(NY, s)) for s in range(1, NY)]
        total = project(c, everyone, weight, total)
    return total


def solution(mesh):
    devices = mesh.devices.reshape(mesh.devices.shape[0], NZ, NX, NY)
    grid = Mesh(devices, ("batch", "z", "x", "head"))
    rows = ("batch", "z", "x")
    in_specs = (
        P(rows, "head"),
        P(rows, None, "head"),
        P("head", None),
        P("batch", None),
        P("batch"),
    )
    return jax.shard_map(
        body, mesh=grid, in_specs=in_specs, out_specs=P(rows, "head"), check_vma=False
    )
```

time: 526 us -> 226 us (0.43)
  waiting for transfers between devices: 289 us -> 57.3 us
  Pallas kernels: 0 us -> 95.2 us
  blocking collectives: 71 us -> 0 us
  local copies, waits for them, and re-layouts: 74 us -> 14.2 us
  other arithmetic: 47 us -> 0.59 us
  starting transfers between devices: 16.2 us -> 58.8 us
  matrix products: 16.4 us -> 0 us
  between operations: 13.4 us -> 0.25 us
    psum x1 -> x0, waiting for transfers between devices: 216 us -> none  [body(): lax.psum(glob_query.astype(jnp.bfloat16), 'ctx').astype(jnp.float32)]
    pallas_call x0 -> x7, Pallas kernels: none -> 95.2 us  [the longest x2 82.6 us: attend(): pl.pallas_call(functools.partial(attend_kernel, chunk), out_shape=[messag...]
    all_gather x2 -> x0, blocking collectives: 71 us -> none  [combined_all(): everything = jax.tree.map(lambda part: lax.all_gather(part, axis), value)]
    reduce_scatter x1 -> x0, waiting for transfers between devices: 68.2 us -> none  [body(): lax.psum_scatter(partial_terms.astype(jnp.bfloat16), 'head', scatter_dime...]
    ppermute x2 -> x34, starting transfers between devices: 6.22 us -> 58.8 us  [the longest x8 23.7 us: ring_step(): lax.ppermute(right, 'z', shift(NZ, 1))]
    ppermute x2 -> x34, waiting for transfers between devices: 5.15 us -> 57.3 us  [the longest x8 30.5 us: ring_step(): lax.ppermute(right, 'z', shift(NZ, 1))]
    add x63 -> x0, other arithmetic: 38.8 us -> none  [the longest x31 37.7 us: combine_rows(): acc_early * factor_early[..., None] + acc_later * factor_later[..., None]]
    gather x6 -> x0, local copies, waits for them, and re-layouts: 36 us -> none  [the longest x2 28.5 us: body(): outgoing = kv_blocks[chosen]]
  transfers between devices with their start and end apart: 6 -> 34, of which waited for: 3 -> 14; matrix products, arithmetic and copies ran while one was open for 10% -> 4% of each run, Pallas kernels for 0% -> 40%
where the time goes in v1:
time: 226 us
  Pallas kernels  95.2 us (42%)
  starting transfers between devices  58.8 us (26%)
  waiting for transfers between devices  57.3 us (25%)
  local copies, waits for them, and re-layouts  14.2 us (6%)
    pallas_call x2, Pallas kernels, attend(): pl.pallas_call(functools.partial(attend_kernel, chunk), out_shape=[messag...  82.6 us
    ppermute x8, waiting for transfers between devices, ring_step(): lax.ppermute(right, 'z', shift(NZ, 1))  30.5 us
    ppermute x8, starting transfers between devices, ring_step(): lax.ppermute(right, 'z', shift(NZ, 1))  23.7 us
    ppermute x6, waiting for transfers between devices, body(): lax.ppermute(att, 'head', shift(NY, s))  17.8 us
    ppermute x6, starting transfers between devices, body(): lax.ppermute(messages[s], 'x', shift(NX, -s))  17.5 us
    ppermute x6, starting transfers between devices, body(): lax.ppermute(att, 'head', shift(NY, s))  8.03 us
    pallas_call x2, Pallas kernels, project(): pl.pallas_call(functools.partial(project_kernel, last), grid=(columns //...  7.84 us
    ppermute x3, starting transfers between devices, body(): weight.append(part if s == 0 else lax.ppermute(part, 'head', shift(NY, s)))  7.47 us
  transfers between devices with their start and end apart: 34, of which 14 were waited for; matrix products, arithmetic and copies ran while one was open for 4% of the time, Pallas kernels for 40%

profile of v1, /device:TPU:103, one launch (start us, length us, event | category | flops | bytes accessed | tf_op | source)
XLA Modules:
  0.0 226.3 jit_solution(5438532460526683354)
XLA Ops:
  1.5 2.9 %collective-permute-start.23 = (bf16[2,512,256]{2,1,0:T(8,128)(2,1)S(1)}, bf16[2,512,256]{2,1,0:T(8,128)(2,1)S(1)}, u32[]{:S(2)}, u32[]{:S(2)}) collective-permute-start(bf16[2,512,256]{2,1,0:T(8,128)(2,1)S(1)} %get-tuple-element.31.refs_7_), channel_id=1, source_target_pairs={{0,16},{16,32},{32,48},{48,64},{64,80},{80,96},{96,112},{112,0},{1... | collective-permute-start | bytes 1572872 | tf_op jit(solution)/shard_map/ppermute | solution.py:329
  5.3 2.7 %collective-permute-start.6 = (bf16[2,512,256]{2,1,0:T(8,128)(2,1)S(1)}, bf16[2,512,256]{2,1,0:T(8,128)(2,1)}, u32[]{:S(2)}, u32[]{:S(2)}) collective-permute-start(bf16[2,512,256]{2,1,0:T(8,128)(2,1)S(1)} %get-tuple-element.32.refs_7_), channel_id=1, source_target_pairs={{0,16},{16,32},{32,48},{48,64},{64,80},{80,96},{96,112},{112,0},{1... | collective-permute-start | bytes 1572872 | tf_op jit(solution)/shard_map/ppermute | solution.py:329
  7.9 7.1 %collective-permute-done.23.refs_13_ = bf16[2,512,256]{2,1,0:T(8,128)(2,1)S(1)} collective-permute-done((bf16[2,512,256]{2,1,0:T(8,128)(2,1)S(1)}, bf16[2,512,256]{2,1,0:T(8,128)(2,1)S(1)}, u32[]{:S(2)}, u32[]{:S(2)}) %collective-permute-start.23) | collective-permute-done | bytes 524320 | tf_op jit(solution)/shard_map/ppermute | solution.py:329
  15.1 3.4 %collective-permute-start.24 = (bf16[2,512,256]{2,1,0:T(8,128)(2,1)S(1)}, bf16[2,512,256]{2,1,0:T(8,128)(2,1)}, u32[]{:S(2)}, u32[]{:S(2)}) collective-permute-start(bf16[2,512,256]{2,1,0:T(8,128)(2,1)S(1)} %collective-permute-done.23.refs_13_), channel_id=1, source_target_pairs={{0,16},{16,32},{32,48},{48,64},{64,80},{80,96},{96,112},{112,0},{1... | collective-permute-start | bytes 1572872 | tf_op jit(solution)/shard_map/ppermute | solution.py:329
  19.1 7.2 %collective-permute-done.6.refs_13_ = bf16[2,512,256]{2,1,0:T(8,128)(2,1)} collective-permute-done((bf16[2,512,256]{2,1,0:T(8,128)(2,1)S(1)}, bf16[2,512,256]{2,1,0:T(8,128)(2,1)}, u32[]{:S(2)}, u32[]{:S(2)}) %collective-permute-start.6) | collective-permute-done | bytes 524320 | tf_op jit(solution)/shard_map/ppermute | solution.py:329
  26.3 3.5 %collective-permute-start.7 = (bf16[2,512,256]{2,1,0:T(8,128)(2,1)}, bf16[2,512,256]{2,1,0:T(8,128)(2,1)}, u32[]{:S(2)}, u32[]{:S(2)}) collective-permute-start(bf16[2,512,256]{2,1,0:T(8,128)(2,1)} %collective-permute-done.6.refs_13_), channel_id=1, source_target_pairs={{0,16},{16,32},{32,48},{48,64},{64,80},{80,96},{96,112},{112,0},{1... | collective-permute-start | bytes 1572872 | tf_op jit(solution)/shard_map/ppermute | solution.py:329
  29.8 7.7 %collective-permute-done.24.refs_12_ = bf16[2,512,256]{2,1,0:T(8,128)(2,1)} collective-permute-done((bf16[2,512,256]{2,1,0:T(8,128)(2,1)S(1)}, bf16[2,512,256]{2,1,0:T(8,128)(2,1)}, u32[]{:S(2)}, u32[]{:S(2)}) %collective-permute-start.24) | collective-permute-done | bytes 524320 | tf_op jit(solution)/shard_map/ppermute | solution.py:329
  37.5 3.5 %collective-permute-start.25 = (bf16[2,512,256]{2,1,0:T(8,128)(2,1)}, bf16[2,512,256]{2,1,0:T(8,128)(2,1)}, u32[]{:S(2)}, u32[]{:S(2)}) collective-permute-start(bf16[2,512,256]{2,1,0:T(8,128)(2,1)} %collective-permute-done.24.refs_12_), channel_id=1, source_target_pairs={{0,16},{16,32},{32,48},{48,64},{64,80},{80,96},{96,112},{112,0},{1... | collective-permute-start | bytes 1572872 | tf_op jit(solution)/shard_map/ppermute | solution.py:329
  41.1 4.0 %constant_dynamic-slice_fusion = (bf16[512,1024]{1,0:T(8,128)(2,1)}, bf16[512,1024]{1,0:T(8,128)(2,1)}, bf16[512,1024]{1,0:T(8,128)(2,1)S(1)}, bf16[512,1024]{1,0:T(8,128)(2,1)}) fusion(bf16[512,4096]{1,0:T(8,128)(2,1)} %param.7, s32[]{:T(128)S(6)} %select_n.38, s32[]{:T(128)S(6)} %select_n.34, s32[]{:T(128)S(6)} %select_n.32, s32[]{:T(128)S(6)} %select_n.36), kind=kLoop, calls=%fused_computation.5 | loop fusion | bytes 8388624 | tf_op jit(solution)/shard_map/dynamic_slice | solution.py:352
  46.3 2.5 %collective-permute-done.7.refs_12_ = bf16[2,512,256]{2,1,0:T(8,128)(2,1)} collective-permute-done((bf16[2,512,256]{2,1,0:T(8,128)(2,1)}, bf16[2,512,256]{2,1,0:T(8,128)(2,1)}, u32[]{:S(2)}, u32[]{:S(2)}) %collective-permute-start.7) | collective-permute-done | bytes 524320 | tf_op jit(solution)/shard_map/ppermute | solution.py:329
  48.9 3.4 %collective-permute-start.8 = (bf16[2,512,256]{2,1,0:T(8,128)(2,1)}, bf16[2,512,256]{2,1,0:T(8,128)(2,1)}, u32[]{:S(2)}, u32[]{:S(2)}) collective-permute-start(bf16[2,512,256]{2,1,0:T(8,128)(2,1)} %collective-permute-done.7.refs_12_), channel_id=1, source_target_pairs={{0,16},{16,32},{32,48},{48,64},{64,80},{80,96},{96,112},{112,0},{1... | collective-permute-start | bytes 1572872 | tf_op jit(solution)/shard_map/ppermute | solution.py:329
  53.8 3.1 %shard_map.55 = (s32[32]{0:T(128)}, s32[264]{0:T(512)}, s32[2]{0:T(128)}) custom-call(s32[768]{0:T(1024)} %reshape.3.table, s32[2]{0:T(128)} %glob.1, s32[2]{0:T(128)} %pad_add_fusion.place), custom_call_target="tpu_custom_call" | custom-call | tf_op jit(solution)/shard_map/pallas_call | solution.py:70
  57.2 2.9 %collective-permute-done.25.refs_11_ = bf16[2,512,256]{2,1,0:T(8,128)(2,1)} collective-permute-done((bf16[2,512,256]{2,1,0:T(8,128)(2,1)}, bf16[2,512,256]{2,1,0:T(8,128)(2,1)}, u32[]{:S(2)}, u32[]{:S(2)}) %collective-permute-start.25) | collective-permute-done | bytes 524320 | tf_op jit(solution)/shard_map/ppermute | solution.py:329
  60.1 2.7 %collective-permute-start.19 = (bf16[512,1024]{1,0:T(8,128)(2,1)}, bf16[512,1024]{1,0:T(8,128)(2,1)S(1)}, u32[]{:S(2)}, u32[]{:S(2)}) collective-permute-start(bf16[512,1024]{1,0:T(8,128)(2,1)} %get-tuple-element.27), channel_id=1, source_target_pairs={{0,3},{1,0},{2,1},{3,2},{4,7},{5,4},{6,5},{7,6},{8,11},{9,8},{10,9... | collective-permute-start | bytes 3145736 | tf_op jit(solution)/shard_map/ppermute | solution.py:353
  65.1 3.1 %collective-permute-start.26 = (bf16[512,256]{1,0:T(8,128)(2,1)S(1)}, bf16[512,256]{1,0:T(8,128)(2,1)S(1)}, u32[]{:S(2)}, u32[]{:S(2)}) collective-permute-start(bf16[512,256]{1,0:T(8,128)(2,1)S(1)} %slice_bitcast_fusion.1), channel_id=1, source_target_pairs={{0,16},{16,32},{32,48},{48,64},{64,80},{80,96},{96,112},{112,0},{1... | collective-permute-start | bytes 786440 | tf_op jit(solution)/shard_map/ppermute | solution.py:329
  68.3 3.1 %collective-permute-done.8.refs_11_ = bf16[2,512,256]{2,1,0:T(8,128)(2,1)} collective-permute-done((bf16[2,512,256]{2,1,0:T(8,128)(2,1)}, bf16[2,512,256]{2,1,0:T(8,128)(2,1)}, u32[]{:S(2)}, u32[]{:S(2)}) %collective-permute-start.8) | collective-permute-done | bytes 524320 | tf_op jit(solution)/shard_map/ppermute | solution.py:329
  75.7 3.4 %collective-permute-start.18 = (bf16[512,1024]{1,0:T(8,128)(2,1)}, bf16[512,1024]{1,0:T(8,128)(2,1)S(1)}, u32[]{:S(2)}, u32[]{:S(2)}) collective-permute-start(bf16[512,1024]{1,0:T(8,128)(2,1)} %get-tuple-element.30), channel_id=1, source_target_pairs={{0,2},{1,3},{2,0},{3,1},{4,6},{5,7},{6,4},{7,5},{8,10},{9,11},{10,... | collective-permute-start | bytes 3145736 | tf_op jit(solution)/shard_map/ppermute | solution.py:353
  85.6 41.3 %shard_map.58 = (bf16[528,256]{1,0:T(8,128)(2,1)S(1)}, bf16[528,256]{1,0:T(8,128)(2,1)S(1)}, bf16[528,256]{1,0:T(8,128)(2,1)S(1)}, bf16[528,256]{1,0:T(8,128)(2,1)S(1)}) custom-call(s32[32]{0:T(128)S(1)} %copy-done.6, s32[264]{0:T(512)S(1)} %copy-done.5, s32[2]{0:T(128)S(1)} %copy-done.7, bf16[512,512]{1,0:T(8,128)(2,1)S(1)} %copy-done, ...), custom_call_target="tpu_custom_call" | custom-call | flops 1500000000 | bytes 8000000 | tf_op jit(solution)/shard_map/pallas_call | solution.py:236
  127.0 6.9 %collective-permute-start.28 = (bf16[528,256]{1,0:T(8,128)(2,1)S(1)}, bf16[528,256]{1,0:T(8,128)(2,1)S(1)}, u32[]{:S(2)}, u32[]{:S(2)}) collective-permute-start(bf16[528,256]{1,0:T(8,128)(2,1)S(1)} %get-tuple-element.24), channel_id=1, source_target_pairs={{0,12},{4,0},{8,4},{12,8},{1,13},{5,1},{9,5},{13,9},{2,14},{6,2},{... | collective-permute-start | bytes 811016 | tf_op jit(solution)/shard_map/ppermute | solution.py:359
  133.9 2.5 %collective-permute-start.30 = (bf16[528,256]{1,0:T(8,128)(2,1)S(1)}, bf16[528,256]{1,0:T(8,128)(2,1)S(1)}, u32[]{:S(2)}, u32[]{:S(2)}) collective-permute-start(bf16[528,256]{1,0:T(8,128)(2,1)S(1)} %get-tuple-element.26), channel_id=1, source_target_pairs={{0,4},{4,8},{8,12},{12,0},{1,5},{5,9},{9,13},{13,1},{2,6},{6,10},{... | collective-permute-start | bytes 811016 | tf_op jit(solution)/shard_map/ppermute | solution.py:359
  136.4 41.3 %shard_map.56 = (bf16[528,256]{1,0:T(8,128)(2,1)S(1)}, bf16[528,256]{1,0:T(8,128)(2,1)S(1)}, bf16[528,256]{1,0:T(8,128)(2,1)S(1)}, bf16[528,256]{1,0:T(8,128)(2,1)S(1)}) custom-call(s32[32]{0:T(128)S(1)} %copy-done.6, s32[264]{0:T(512)S(1)} %copy-done.5, s32[2]{0:T(128)S(1)} %copy-done.7, bf16[512,512]{1,0:T(8,128)(2,1)S(1)} %copy-done, ...), custom_call_target="tpu_custom_call" | custom-call | flops 1500000000 | bytes 8000000 | tf_op jit(solution)/shard_map/pallas_call | solution.py:236
  177.7 5.4 %collective-permute-start.11 = (bf16[528,256]{1,0:T(8,128)(2,1)S(1)}, bf16[528,256]{1,0:T(8,128)(2,1)S(1)}, u32[]{:S(2)}, u32[]{:S(2)}) collective-permute-start(bf16[528,256]{1,0:T(8,128)(2,1)S(1)} %get-tuple-element.20), channel_id=1, source_target_pairs={{0,12},{4,0},{8,4},{12,8},{1,13},{5,1},{9,5},{13,9},{2,14},{6,2},{... | collective-permute-start | bytes 811016 | tf_op jit(solution)/shard_map/ppermute | solution.py:359
  183.1 2.7 %collective-permute-start.13 = (bf16[528,256]{1,0:T(8,128)(2,1)S(1)}, bf16[528,256]{1,0:T(8,128)(2,1)S(1)}, u32[]{:S(2)}, u32[]{:S(2)}) collective-permute-start(bf16[528,256]{1,0:T(8,128)(2,1)S(1)} %get-tuple-element.22), channel_id=1, source_target_pairs={{0,4},{4,8},{8,12},{12,0},{1,5},{5,9},{9,13},{13,1},{2,6},{6,10},{... | collective-permute-start | bytes 811016 | tf_op jit(solution)/shard_map/ppermute | solution.py:359
  186.6 5.1 %collective-permute-done.11.m1 = bf16[528,256]{1,0:T(8,128)(2,1)S(1)} collective-permute-done((bf16[528,256]{1,0:T(8,128)(2,1)S(1)}, bf16[528,256]{1,0:T(8,128)(2,1)S(1)}, u32[]{:S(2)}, u32[]{:S(2)}) %collective-permute-start.11) | collective-permute-done | bytes 270368 | tf_op jit(solution)/shard_map/ppermute | solution.py:359
  191.7 3.5 %collective-permute-start.33 = (bf16[512,256]{1,0:T(8,128)(2,1)S(1)}, bf16[512,256]{1,0:T(8,128)(2,1)S(1)}, u32[]{:S(2)}, u32[]{:S(2)}) collective-permute-start(bf16[512,256]{1,0:T(8,128)(2,1)S(1)} %shard_map.59.refs_0_), channel_id=1, source_target_pairs={{0,3},{1,0},{2,1},{3,2},{4,7},{5,4},{6,5},{7,6},{8,11},{9,8},{10,9... | collective-permute-start | bytes 786440 | tf_op jit(solution)/shard_map/ppermute | solution.py:362
  197.1 2.6 %collective-permute-start.16 = (bf16[512,256]{1,0:T(8,128)(2,1)S(1)}, bf16[512,256]{1,0:T(8,128)(2,1)S(1)}, u32[]{:S(2)}, u32[]{:S(2)}) collective-permute-start(bf16[512,256]{1,0:T(8,128)(2,1)S(1)} %shard_map.57.refs_0_), channel_id=1, source_target_pairs={{0,3},{1,0},{2,1},{3,2},{4,7},{5,4},{6,5},{7,6},{8,11},{9,8},{10,9... | collective-permute-start | bytes 786440 | tf_op jit(solution)/shard_map/ppermute | solution.py:362
  200.6 4.6 %collective-permute-done.33.refs_3_ = bf16[512,256]{1,0:T(8,128)(2,1)S(1)} collective-permute-done((bf16[512,256]{1,0:T(8,128)(2,1)S(1)}, bf16[512,256]{1,0:T(8,128)(2,1)S(1)}, u32[]{:S(2)}, u32[]{:S(2)}) %collective-permute-start.33) | collective-permute-done | bytes 262176 | tf_op jit(solution)/shard_map/ppermute | solution.py:362
  205.2 6.1 %collective-permute-done.31.refs_1_ = bf16[512,256]{1,0:T(8,128)(2,1)S(1)} collective-permute-done((bf16[512,256]{1,0:T(8,128)(2,1)S(1)}, bf16[512,256]{1,0:T(8,128)(2,1)S(1)}, u32[]{:S(2)}, u32[]{:S(2)}) %collective-permute-start.31) | collective-permute-done | bytes 262176 | tf_op jit(solution)/shard_map/ppermute | solution.py:362
  211.3 3.3 %shard_map.60.refs_8_ = f32[512,1024]{1,0:T(8,128)} custom-call(bf16[512,256]{1,0:T(8,128)(2,1)S(1)} %shard_map.59.refs_0_, bf16[512,256]{1,0:T(8,128)(2,1)S(1)} %collective-permute-done.31.refs_1_, bf16[512,256]{1,0:T(8,128)(2,1)S(1)} %collective-permute-done.32.refs_2_, bf16[512,256]{1,0:T(8,128)(2,1)S(1)} %collective-permute-done.33.refs_3_, ...), custom_call_target="tpu_custom_call" | custom-call | flops 1073741824 | bytes 5000000 | tf_op jit(solution)/shard_map/pallas_call | solution.py:312
  214.6 2.9 %collective-permute-done.16.refs_3_ = bf16[512,256]{1,0:T(8,128)(2,1)S(1)} collective-permute-done((bf16[512,256]{1,0:T(8,128)(2,1)S(1)}, bf16[512,256]{1,0:T(8,128)(2,1)S(1)}, u32[]{:S(2)}, u32[]{:S(2)}) %collective-permute-start.16) | collective-permute-done | bytes 262176 | tf_op jit(solution)/shard_map/ppermute | solution.py:362
  217.5 4.2 %collective-permute-done.14.refs_1_ = bf16[512,256]{1,0:T(8,128)(2,1)S(1)} collective-permute-done((bf16[512,256]{1,0:T(8,128)(2,1)S(1)}, bf16[512,256]{1,0:T(8,128)(2,1)S(1)}, u32[]{:S(2)}, u32[]{:S(2)}) %collective-permute-start.14) | collective-permute-done | bytes 262176 | tf_op jit(solution)/shard_map/ppermute | solution.py:362
  221.7 4.6 %shard_map.61 = bf16[512,1024]{1,0:T(8,128)(2,1)} custom-call(bf16[512,256]{1,0:T(8,128)(2,1)S(1)} %shard_map.57.refs_0_, bf16[512,256]{1,0:T(8,128)(2,1)S(1)} %collective-permute-done.14.refs_1_, bf16[512,256]{1,0:T(8,128)(2,1)S(1)} %collective-permute-done.15.refs_2_, bf16[512,256]{1,0:T(8,128)(2,1)S(1)} %collective-permute-done.16.refs_3_, ...), custom_call_target="tpu_custom_call" | custom-call | flops 1073741824 | bytes 5000000 | tf_op jit(solution)/shard_map/pallas_call | solution.py:312
  (73 shorter events, 22.8 us)
Async XLA Ops:
  1.5 13.5 %collective-permute-start.23 = (bf16[2,512,256]{2,1,0:T(8,128)(2,1)S(1)}, bf16[2,512,256]{2,1,0:T(8,128)(2,1)S(1)}, u32[]{:S(2)}, u32[]{:S(2)}) collective-permute-start(bf16[2,512,256]{2,1,0:T(8,128)(2,1)S(1)} %get-tuple-element.31.refs_7_), channel_id=1, source_target_pairs={{0,16},{16,32},{32,48},{48,64},{64,80},{80,96},{96,112},{112,0},{1... | collective-permute-start | bytes 1572872 | tf_op jit(solution)/shard_map/ppermute | solution.py:329
  4.5 14.0 %collective-permute-start.20 = (bf16[2,512,256]{2,1,0:T(8,128)(2,1)S(1)}, bf16[2,512,256]{2,1,0:T(8,128)(2,1)S(1)}, u32[]{:S(2)}, u32[]{:S(2)}) collective-permute-start(bf16[2,512,256]{2,1,0:T(8,128)(2,1)S(1)} %get-tuple-element.31.refs_7_), channel_id=1, source_target_pairs={{0,112},{16,0},{32,16},{48,32},{64,48},{80,64},{96,80},{112,96},{1... | collective-permute-start | bytes 1572872 | tf_op jit(solution)/shard_map/ppermute | solution.py:330
  5.3 21.0 %collective-permute-start.6 = (bf16[2,512,256]{2,1,0:T(8,128)(2,1)S(1)}, bf16[2,512,256]{2,1,0:T(8,128)(2,1)}, u32[]{:S(2)}, u32[]{:S(2)}) collective-permute-start(bf16[2,512,256]{2,1,0:T(8,128)(2,1)S(1)} %get-tuple-element.32.refs_7_), channel_id=1, source_target_pairs={{0,16},{16,32},{32,48},{48,64},{64,80},{80,96},{96,112},{112,0},{1... | collective-permute-start | bytes 1572872 | tf_op jit(solution)/shard_map/ppermute | solution.py:329
  7.9 21.9 %collective-permute-start.3 = (bf16[2,512,256]{2,1,0:T(8,128)(2,1)S(1)}, bf16[2,512,256]{2,1,0:T(8,128)(2,1)}, u32[]{:S(2)}, u32[]{:S(2)}) collective-permute-start(bf16[2,512,256]{2,1,0:T(8,128)(2,1)S(1)} %get-tuple-element.32.refs_7_), channel_id=1, source_target_pairs={{0,112},{16,0},{32,16},{48,32},{64,48},{80,64},{96,80},{112,96},{1... | collective-permute-start | bytes 1572872 | tf_op jit(solution)/shard_map/ppermute | solution.py:330
  15.1 22.5 %collective-permute-start.24 = (bf16[2,512,256]{2,1,0:T(8,128)(2,1)S(1)}, bf16[2,512,256]{2,1,0:T(8,128)(2,1)}, u32[]{:S(2)}, u32[]{:S(2)}) collective-permute-start(bf16[2,512,256]{2,1,0:T(8,128)(2,1)S(1)} %collective-permute-done.23.refs_13_), channel_id=1, source_target_pairs={{0,16},{16,32},{32,48},{48,64},{64,80},{80,96},{96,112},{112,0},{1... | collective-permute-start | bytes 1572872 | tf_op jit(solution)/shard_map/ppermute | solution.py:329
  18.5 22.6 %collective-permute-start.21 = (bf16[2,512,256]{2,1,0:T(8,128)(2,1)S(1)}, bf16[2,512,256]{2,1,0:T(8,128)(2,1)}, u32[]{:S(2)}, u32[]{:S(2)}) collective-permute-start(bf16[2,512,256]{2,1,0:T(8,128)(2,1)S(1)} %collective-permute-done.20.refs_8_), channel_id=1, source_target_pairs={{0,112},{16,0},{32,16},{48,32},{64,48},{80,64},{96,80},{112,96},{1... | collective-permute-start | bytes 1572872 | tf_op jit(solution)/shard_map/ppermute | solution.py:330
  18.5 26.6 %collective-permute-start.2 = (bf16[512,512]{1,0:T(8,128)(2,1)S(1)}, bf16[512,512]{1,0:T(8,128)(2,1)S(1)}, u32[]{:S(2)}, u32[]{:S(2)}) collective-permute-start(bf16[512,512]{1,0:T(8,128)(2,1)S(1)} %copy-done), channel_id=1, source_target_pairs={{0,12},{4,0},{8,4},{12,8},{1,13},{5,1},{9,5},{13,9},{2,14},{6,2},{... | collective-permute-start | bytes 1572872 | tf_op jit(solution)/shard_map/ppermute | solution.py:348
  26.3 22.6 %collective-permute-start.7 = (bf16[2,512,256]{2,1,0:T(8,128)(2,1)}, bf16[2,512,256]{2,1,0:T(8,128)(2,1)}, u32[]{:S(2)}, u32[]{:S(2)}) collective-permute-start(bf16[2,512,256]{2,1,0:T(8,128)(2,1)} %collective-permute-done.6.refs_13_), channel_id=1, source_target_pairs={{0,16},{16,32},{32,48},{48,64},{64,80},{80,96},{96,112},{112,0},{1... | collective-permute-start | bytes 1572872 | tf_op jit(solution)/shard_map/ppermute | solution.py:329
  29.8 27.1 %collective-permute-start.4 = (bf16[2,512,256]{2,1,0:T(8,128)(2,1)}, bf16[2,512,256]{2,1,0:T(8,128)(2,1)}, u32[]{:S(2)}, u32[]{:S(2)}) collective-permute-start(bf16[2,512,256]{2,1,0:T(8,128)(2,1)} %collective-permute-done.3.refs_8_), channel_id=1, source_target_pairs={{0,112},{16,0},{32,16},{48,32},{64,48},{80,64},{96,80},{112,96},{1... | collective-permute-start | bytes 1572872 | tf_op jit(solution)/shard_map/ppermute | solution.py:330
  37.5 22.6 %collective-permute-start.25 = (bf16[2,512,256]{2,1,0:T(8,128)(2,1)}, bf16[2,512,256]{2,1,0:T(8,128)(2,1)}, u32[]{:S(2)}, u32[]{:S(2)}) collective-permute-start(bf16[2,512,256]{2,1,0:T(8,128)(2,1)} %collective-permute-done.24.refs_12_), channel_id=1, source_target_pairs={{0,16},{16,32},{32,48},{48,64},{64,80},{80,96},{96,112},{112,0},{1... | collective-permute-start | bytes 1572872 | tf_op jit(solution)/shard_map/ppermute | solution.py:329
  41.0 22.1 %collective-permute-start.22 = (bf16[2,512,256]{2,1,0:T(8,128)(2,1)}, bf16[2,512,256]{2,1,0:T(8,128)(2,1)}, u32[]{:S(2)}, u32[]{:S(2)}) collective-permute-start(bf16[2,512,256]{2,1,0:T(8,128)(2,1)} %collective-permute-done.21.refs_9_), channel_id=1, source_target_pairs={{0,112},{16,0},{32,16},{48,32},{64,48},{80,64},{96,80},{112,96},{1... | collective-permute-start | bytes 1572872 | tf_op jit(solution)/shard_map/ppermute | solution.py:330
  45.1 20.0 %collective-permute-start.1 = (bf16[512,512]{1,0:T(8,128)(2,1)S(1)}, bf16[512,512]{1,0:T(8,128)(2,1)S(1)}, u32[]{:S(2)}, u32[]{:S(2)}) collective-permute-start(bf16[512,512]{1,0:T(8,128)(2,1)S(1)} %copy-done), channel_id=1, source_target_pairs={{0,8},{4,12},{8,0},{12,4},{1,9},{5,13},{9,1},{13,5},{2,10},{6,14},... | collective-permute-start | bytes 1572872 | tf_op jit(solution)/shard_map/ppermute | solution.py:348
  48.9 22.5 %collective-permute-start.8 = (bf16[2,512,256]{2,1,0:T(8,128)(2,1)}, bf16[2,512,256]{2,1,0:T(8,128)(2,1)}, u32[]{:S(2)}, u32[]{:S(2)}) collective-permute-start(bf16[2,512,256]{2,1,0:T(8,128)(2,1)} %collective-permute-done.7.refs_12_), channel_id=1, source_target_pairs={{0,16},{16,32},{32,48},{48,64},{64,80},{80,96},{96,112},{112,0},{1... | collective-permute-start | bytes 1572872 | tf_op jit(solution)/shard_map/ppermute | solution.py:329
  56.9 15.4 %collective-permute-start = (bf16[512,512]{1,0:T(8,128)(2,1)S(1)}, bf16[512,512]{1,0:T(8,128)(2,1)S(1)}, u32[]{:S(2)}, u32[]{:S(2)}) collective-permute-start(bf16[512,512]{1,0:T(8,128)(2,1)S(1)} %copy-done), channel_id=1, source_target_pairs={{0,4},{4,8},{8,12},{12,0},{1,5},{5,9},{9,13},{13,1},{2,6},{6,10},{... | collective-permute-start | bytes 1572872 | tf_op jit(solution)/shard_map/ppermute | solution.py:348
  60.1 66.9 %collective-permute-start.19 = (bf16[512,1024]{1,0:T(8,128)(2,1)}, bf16[512,1024]{1,0:T(8,128)(2,1)S(1)}, u32[]{:S(2)}, u32[]{:S(2)}) collective-permute-start(bf16[512,1024]{1,0:T(8,128)(2,1)} %get-tuple-element.27), channel_id=1, source_target_pairs={{0,3},{1,0},{2,1},{3,2},{4,7},{5,4},{6,5},{7,6},{8,11},{9,8},{10,9... | collective-permute-start | bytes 3145736 | tf_op jit(solution)/shard_map/ppermute | solution.py:353
  63.2 12.5 %collective-permute-start.5 = (bf16[2,512,256]{2,1,0:T(8,128)(2,1)}, bf16[2,512,256]{2,1,0:T(8,128)(2,1)S(1)}, u32[]{:S(2)}, u32[]{:S(2)}) collective-permute-start(bf16[2,512,256]{2,1,0:T(8,128)(2,1)} %collective-permute-done.4.refs_9_), channel_id=1, source_target_pairs={{0,112},{16,0},{32,16},{48,32},{64,48},{80,64},{96,80},{112,96},{1... | collective-permute-start | bytes 1572872 | tf_op jit(solution)/shard_map/ppermute | solution.py:330
  65.1 14.0 %collective-permute-start.26 = (bf16[512,256]{1,0:T(8,128)(2,1)S(1)}, bf16[512,256]{1,0:T(8,128)(2,1)S(1)}, u32[]{:S(2)}, u32[]{:S(2)}) collective-permute-start(bf16[512,256]{1,0:T(8,128)(2,1)S(1)} %slice_bitcast_fusion.1), channel_id=1, source_target_pairs={{0,16},{16,32},{32,48},{48,64},{64,80},{80,96},{96,112},{112,0},{1... | collective-permute-start | bytes 786440 | tf_op jit(solution)/shard_map/ppermute | solution.py:329
  72.3 124.7 %collective-permute-start.17 = (bf16[512,1024]{1,0:T(8,128)(2,1)}, bf16[512,1024]{1,0:T(8,128)(2,1)S(1)}, u32[]{:S(2)}, u32[]{:S(2)}) collective-permute-start(bf16[512,1024]{1,0:T(8,128)(2,1)} %get-tuple-element.28), channel_id=1, source_target_pairs={{0,1},{1,2},{2,3},{3,0},{4,5},{5,6},{6,7},{7,4},{8,9},{9,10},{10,1... | collective-permute-start | bytes 3145736 | tf_op jit(solution)/shard_map/ppermute | solution.py:353
  75.7 124.0 %collective-permute-start.18 = (bf16[512,1024]{1,0:T(8,128)(2,1)}, bf16[512,1024]{1,0:T(8,128)(2,1)S(1)}, u32[]{:S(2)}, u32[]{:S(2)}) collective-permute-start(bf16[512,1024]{1,0:T(8,128)(2,1)} %get-tuple-element.30), channel_id=1, source_target_pairs={{0,2},{1,3},{2,0},{3,1},{4,6},{5,7},{6,4},{7,5},{8,10},{9,11},{10,... | collective-permute-start | bytes 3145736 | tf_op jit(solution)/shard_map/ppermute | solution.py:353
  79.1 54.8 %collective-permute-start.9 = (bf16[512,256]{1,0:T(8,128)(2,1)S(1)}, bf16[512,256]{1,0:T(8,128)(2,1)S(1)}, u32[]{:S(2)}, u32[]{:S(2)}) collective-permute-start(bf16[512,256]{1,0:T(8,128)(2,1)S(1)} %slice_bitcast_fusion.3), channel_id=1, source_target_pairs={{0,16},{16,32},{32,48},{48,64},{64,80},{80,96},{96,112},{112,0},{1... | collective-permute-start | bytes 786440 | tf_op jit(solution)/shard_map/ppermute | solution.py:329
  81.7 52.2 %collective-permute-start.10 = (bf16[512,256]{1,0:T(8,128)(2,1)S(1)}, bf16[512,256]{1,0:T(8,128)(2,1)S(1)}, u32[]{:S(2)}, u32[]{:S(2)}) collective-permute-start(bf16[512,256]{1,0:T(8,128)(2,1)S(1)} %slice_bitcast_fusion.2), channel_id=1, source_target_pairs={{0,112},{16,0},{32,16},{48,32},{64,48},{80,64},{96,80},{112,96},{1... | collective-permute-start | bytes 786440 | tf_op jit(solution)/shard_map/ppermute | solution.py:330
  127.0 50.7 %collective-permute-start.28 = (bf16[528,256]{1,0:T(8,128)(2,1)S(1)}, bf16[528,256]{1,0:T(8,128)(2,1)S(1)}, u32[]{:S(2)}, u32[]{:S(2)}) collective-permute-start(bf16[528,256]{1,0:T(8,128)(2,1)S(1)} %get-tuple-element.24), channel_id=1, source_target_pairs={{0,12},{4,0},{8,4},{12,8},{1,13},{5,1},{9,5},{13,9},{2,14},{6,2},{... | collective-permute-start | bytes 811016 | tf_op jit(solution)/shard_map/ppermute | solution.py:359
  133.9 49.2 %collective-permute-start.29 = (bf16[528,256]{1,0:T(8,128)(2,1)S(1)}, bf16[528,256]{1,0:T(8,128)(2,1)S(1)}, u32[]{:S(2)}, u32[]{:S(2)}) collective-permute-start(bf16[528,256]{1,0:T(8,128)(2,1)S(1)} %get-tuple-element.25), channel_id=1, source_target_pairs={{0,8},{4,12},{8,0},{12,4},{1,9},{5,13},{9,1},{13,5},{2,10},{6,14},... | collective-permute-start | bytes 811016 | tf_op jit(solution)/shard_map/ppermute | solution.py:359
  133.9 49.2 %collective-permute-start.30 = (bf16[528,256]{1,0:T(8,128)(2,1)S(1)}, bf16[528,256]{1,0:T(8,128)(2,1)S(1)}, u32[]{:S(2)}, u32[]{:S(2)}) collective-permute-start(bf16[528,256]{1,0:T(8,128)(2,1)S(1)} %get-tuple-element.26), channel_id=1, source_target_pairs={{0,4},{4,8},{8,12},{12,0},{1,5},{5,9},{9,13},{13,1},{2,6},{6,10},{... | collective-permute-start | bytes 811016 | tf_op jit(solution)/shard_map/ppermute | solution.py:359
  177.7 14.0 %collective-permute-start.11 = (bf16[528,256]{1,0:T(8,128)(2,1)S(1)}, bf16[528,256]{1,0:T(8,128)(2,1)S(1)}, u32[]{:S(2)}, u32[]{:S(2)}) collective-permute-start(bf16[528,256]{1,0:T(8,128)(2,1)S(1)} %get-tuple-element.20), channel_id=1, source_target_pairs={{0,12},{4,0},{8,4},{12,8},{1,13},{5,1},{9,5},{13,9},{2,14},{6,2},{... | collective-permute-start | bytes 811016 | tf_op jit(solution)/shard_map/ppermute | solution.py:359
  183.1 12.2 %collective-permute-start.12 = (bf16[528,256]{1,0:T(8,128)(2,1)S(1)}, bf16[528,256]{1,0:T(8,128)(2,1)S(1)}, u32[]{:S(2)}, u32[]{:S(2)}) collective-permute-start(bf16[528,256]{1,0:T(8,128)(2,1)S(1)} %get-tuple-element.21), channel_id=1, source_target_pairs={{0,8},{4,12},{8,0},{12,4},{1,9},{5,13},{9,1},{13,5},{2,10},{6,14},... | collective-permute-start | bytes 811016 | tf_op jit(solution)/shard_map/ppermute | solution.py:359
  183.1 13.0 %collective-permute-start.13 = (bf16[528,256]{1,0:T(8,128)(2,1)S(1)}, bf16[528,256]{1,0:T(8,128)(2,1)S(1)}, u32[]{:S(2)}, u32[]{:S(2)}) collective-permute-start(bf16[528,256]{1,0:T(8,128)(2,1)S(1)} %get-tuple-element.22), channel_id=1, source_target_pairs={{0,4},{4,8},{8,12},{12,0},{1,5},{5,9},{9,13},{13,1},{2,6},{6,10},{... | collective-permute-start | bytes 811016 | tf_op jit(solution)/shard_map/ppermute | solution.py:359
  191.7 13.5 %collective-permute-start.33 = (bf16[512,256]{1,0:T(8,128)(2,1)S(1)}, bf16[512,256]{1,0:T(8,128)(2,1)S(1)}, u32[]{:S(2)}, u32[]{:S(2)}) collective-permute-start(bf16[512,256]{1,0:T(8,128)(2,1)S(1)} %shard_map.59.refs_0_), channel_id=1, source_target_pairs={{0,3},{1,0},{2,1},{3,2},{4,7},{5,4},{6,5},{7,6},{8,11},{9,8},{10,9... | collective-permute-start | bytes 786440 | tf_op jit(solution)/shard_map/ppermute | solution.py:362
  196.1 15.3 %collective-permute-start.31 = (bf16[512,256]{1,0:T(8,128)(2,1)S(1)}, bf16[512,256]{1,0:T(8,128)(2,1)S(1)}, u32[]{:S(2)}, u32[]{:S(2)}) collective-permute-start(bf16[512,256]{1,0:T(8,128)(2,1)S(1)} %shard_map.59.refs_0_), channel_id=1, source_target_pairs={{0,1},{1,2},{2,3},{3,0},{4,5},{5,6},{6,7},{7,4},{8,9},{9,10},{10,1... | collective-permute-start | bytes 786440 | tf_op jit(solution)/shard_map/ppermute | solution.py:362
  197.1 20.5 %collective-permute-start.16 = (bf16[512,256]{1,0:T(8,128)(2,1)S(1)}, bf16[512,256]{1,0:T(8,128)(2,1)S(1)}, u32[]{:S(2)}, u32[]{:S(2)}) collective-permute-start(bf16[512,256]{1,0:T(8,128)(2,1)S(1)} %shard_map.57.refs_0_), channel_id=1, source_target_pairs={{0,3},{1,0},{2,1},{3,2},{4,7},{5,4},{6,5},{7,6},{8,11},{9,8},{10,9... | collective-permute-start | bytes 786440 | tf_op jit(solution)/shard_map/ppermute | solution.py:362
  199.7 17.8 %collective-permute-start.15 = (bf16[512,256]{1,0:T(8,128)(2,1)S(1)}, bf16[512,256]{1,0:T(8,128)(2,1)S(1)}, u32[]{:S(2)}, u32[]{:S(2)}) collective-permute-start(bf16[512,256]{1,0:T(8,128)(2,1)S(1)} %shard_map.57.refs_0_), channel_id=1, source_target_pairs={{0,2},{1,3},{2,0},{3,1},{4,6},{5,7},{6,4},{7,5},{8,10},{9,11},{10,... | collective-permute-start | bytes 786440 | tf_op jit(solution)/shard_map/ppermute | solution.py:362
  205.2 16.5 %collective-permute-start.14 = (bf16[512,256]{1,0:T(8,128)(2,1)S(1)}, bf16[512,256]{1,0:T(8,128)(2,1)S(1)}, u32[]{:S(2)}, u32[]{:S(2)}) collective-permute-start(bf16[512,256]{1,0:T(8,128)(2,1)S(1)} %shard_map.57.refs_0_), channel_id=1, source_target_pairs={{0,1},{1,2},{2,3},{3,0},{4,5},{5,6},{6,7},{7,4},{8,9},{9,10},{10,1... | collective-permute-start | bytes 786440 | tf_op jit(solution)/shard_map/ppermute | solution.py:362
  (12 other events, 107.9 us)

commit v2 on v1

v2 whole, which is shorter than its diff:
```python
import functools
import math

import jax
import jax.numpy as jnp
from jax import lax
from jax.experimental import pallas as pl
from jax.experimental.pallas import tpu as pltpu
from jax.sharding import Mesh
from jax.sharding import PartitionSpec as P

DH = 128
BLK = 64
NEG = -1e30
NZ = 8
NX = 4
NY = 4
BPD = 8
TOK = BLK * BPD
HEADS = 4
ALL = HEADS * DH
PAIR = 2
WIDE = PAIR * DH
STAT = 16
GROUP = 4
QBS = NX * BPD
COUNT, LISTED, ORDER = QBS, QBS * 8 + 8, QBS + 8
INDEX_AT = 2 * COUNT
ORDER_AT = INDEX_AT + 2 * LISTED
DENSE_AT = ORDER_AT + 2 * ORDER
X_AT = DENSE_AT + 2
PLAN = X_AT + 1
STAGES = ((0, 1, 2, 6, 7), (3, 4, 5))
SLOTS = [stage * 8 + part.index(p) for p in range(8) for stage, part in enumerate(STAGES) if p in part]
COUNT, LISTED, ORDER = QBS, QBS * 8 + 8, QBS + 8
INDEX_AT = len(STAGES) * COUNT
ORDER_AT = INDEX_AT + len(STAGES) * LISTED
DENSE_AT = ORDER_AT + len(STAGES) * ORDER
X_AT = DENSE_AT + 2
PLAN = X_AT + 1
SCALE = 1.0 / math.sqrt(DH)
SCALE2 = SCALE / math.log(2.0)
VMEM = 28 * 1024 * 1024

any_space = pl.BlockSpec(memory_space=pl.ANY)
in_vmem = pl.BlockSpec(memory_space=pltpu.VMEM)
in_smem = pl.BlockSpec(memory_space=pltpu.SMEM)


def shift(count, by):
    return [(i, (i + by) % count) for i in range(count)]


def plan_kernel(table, glob, place, slots, plan):
    z, x = place[0], place[1]
    plan[X_AT] = x
    for g in range(2):
        owner = glob[g] >> 3
        slot = (x - (owner & 3)) & 3
        plan[DENSE_AT + g] = jnp.where((owner >> 2) == z, slot * BPD + (glob[g] & 7), -1)

    def one(qb, carry):
        qx = (x - (qb >> 3)) & 3
        block = ((z * NX + qx) << 3) + (qb & 7)
        entries = [(block - 1, block > 0), (block, None)]
        entries += [(block + 1, block < NZ * NX * BPD - 1)]
        entries += [(glob[0], None), (glob[1], None)]
        entries += [(table[block * 3 + j], None) for j in range(3)]
        for stage in range(len(STAGES)):
            plan[stage * COUNT + qb] = 0
            for k in range(8):
                plan[INDEX_AT + stage * LISTED + qb * 8 + k] = 0
        for key, exists in entries:
            key = jnp.clip(key, 0, NZ * NX * BPD - 1)
            owner = key >> 3
            here = (owner & 3) == x
            if exists is not None:
                here = here & exists
            slot = slots[((owner >> 2) - z) & 7]
            stage, slot = slot >> 3, slot & 7
            filled = plan[stage * COUNT + qb]
            plan[INDEX_AT + stage * LISTED + qb * 8 + filled] = (slot << 3) + (key & 7)
            plan[stage * COUNT + qb] = filled + here.astype(jnp.int32)
        is_global = (block == glob[0]) | (block == glob[1])
        for stage in range(len(STAGES)):
            plan[stage * COUNT + qb] = jnp.where(is_global, 0, plan[stage * COUNT + qb])
        return carry

    lax.fori_loop(0, QBS, one, 0)

    def place_one(stage, pairs, qb, filled):
        plan[filled] = qb
        return filled + (((plan[stage * COUNT + qb] + 1) >> 1) == pairs).astype(jnp.int32)

    for stage in range(len(STAGES)):
        filled = jnp.int32(ORDER_AT + stage * ORDER)
        for pairs in range(4, -1, -1):
            filled = lax.fori_loop(0, QBS, functools.partial(place_one, stage, pairs), filled)


def make_plan(table, glob, place):
    return pl.pallas_call(
        plan_kernel,
        out_shape=jax.ShapeDtypeStruct((PLAN,), jnp.int32),
        in_specs=[in_smem] * 4,
        out_specs=in_smem,
        compiler_params=pltpu.CompilerParams(vmem_limit_bytes=1024 * 1024),
    )(table, glob, place, jnp.array(SLOTS, jnp.int32))


def dot_t(a, b):
    return lax.dot_general(a, b, (((1,), (1,)), ((), ())), preferred_element_type=jnp.float32)


def attend_kernel(stage, *refs):
    plan, q_in, own_q = refs[:3]
    o_s, stat, q_s, kv_s, wide, sems = refs[-6:]
    slots = kv_s.shape[0]
    copies = [(own_q, q_s.at[0])]
    copies += [(q_in.at[(plan[X_AT] - s) & 3], q_s.at[s]) for s in range(1, NX)]
    out, at_ref = [], 3
    for slot, piece in enumerate(STAGES[stage]):
        if piece == NZ // 2:
            copies += [(refs[at_ref + k], kv_s.at[slot, k]) for k in range(2)]
        else:
            copies.append((refs[at_ref], kv_s.at[slot]))
        at_ref += 2 if piece == NZ // 2 else 1
    if stage > 0:
        copies += [(refs[at_ref], o_s), (refs[at_ref + 1], stat)]
        at_ref += 2
    last = stage == len(STAGES) - 1
    if last:
        for c in range(HEADS // PAIR):
            for s in range(NX):
                part = o_s.at[s, :, pl.ds(c * WIDE, WIDE)]
                out.append((part, refs[at_ref + c * NX + s]))
    else:
        out = [(o_s, refs[at_ref]), (stat, refs[at_ref + 1])]
    copies = [pltpu.make_async_copy(a, b, sems.at[n]) for n, (a, b) in enumerate(copies)]
    for copy in copies:
        copy.start()
    for copy in copies:
        copy.wait()

    def share(top, both):
        total = both[:, DH:]
        return both[:, :DH] / total, top * SCALE + jnp.log(total)

    def at(qb, head):
        rows = pl.ds(pl.multiple_of((qb & 7) * BLK, BLK), BLK)
        return (qb >> 3, rows, slice(head * DH, (head + 1) * DH)), (
            head,
            pl.ds(pl.multiple_of(qb * BLK, BLK), BLK),
            slice(None),
        )

    def merge(qb, head, part, lse):
        if stage == 0:
            return part.astype(jnp.bfloat16), lse
        here, line = at(qb, head)
        before = stat[line]
        top = jnp.maximum(before, lse)
        old, new = jnp.exp(before - top), jnp.exp(lse - top)
        both = old + new
        part = (o_s[here].astype(jnp.float32) * old + part * new) / both
        return part.astype(jnp.bfloat16), top + jnp.log(both)

    def finish(qb, head, part, lse):
        here, line = at(qb, head)
        o_s[here] = part
        stat[line] = lse

    def load_q(qb, head):
        rows = pl.ds(pl.multiple_of((qb & 7) * BLK, BLK), BLK)
        return q_s[qb >> 3, rows, head * DH : (head + 1) * DH]

    lane = lax.broadcasted_iota(jnp.int32, (BLK, 2 * BLK), 1)

    def group(g, pairs):
        blocks = [plan[ORDER_AT + stage * ORDER + g * GROUP + i] for i in range(GROUP)]
        counts = [plan[stage * COUNT + qb] for qb in blocks]
        where = []
        for i in range(GROUP):
            first = INDEX_AT + stage * LISTED + blocks[i] * 8
            entries = [plan[first + e] for e in range(2 * pairs)]
            where.append(
                [(e >> 3, pl.ds(pl.multiple_of((e & 7) * BLK, BLK), BLK)) for e in entries]
            )

        def load(i, h, t, kind):
            cols = slice(h * DH, (h + 1) * DH)
            both = [kv_s[piece, kind, rows, cols] for piece, rows in where[i][2 * t : 2 * t + 2]]
            return jnp.concatenate(both, axis=0)

        chains = [(i, h) for i in range(GROUP) for h in range(HEADS)]
        queries = [load_q(blocks[i], h) for i, h in chains]
        scores = [
            [
                jnp.where(
                    lane < (counts[i] - 2 * t) * BLK, dot_t(query, load(i, h, t, 0)), NEG
                )
                for t in range(pairs)
            ]
            for query, (i, h) in zip(queries, chains)
        ]
        tops = [
            jnp.max(functools.reduce(jnp.maximum, tiles), axis=1, keepdims=True)
            for tiles in scores
        ]
        weights = [
            [jnp.exp2((tile - top) * SCALE2).astype(jnp.bfloat16) for tile in tiles]
            for tiles, top in zip(scores, tops)
        ]
        sums = []
        for (i, h), tiles in zip(chains, weights):
            both = None
            for t in range(pairs):
                values = load(i, h, t, 1)
                values = jnp.concatenate([values, jnp.ones_like(values)], axis=1)
                term = jnp.dot(tiles[t], values, preferred_element_type=jnp.float32)
                both = term if both is None else both + term
            sums.append(both)
        shares = [share(top, both) for top, both in zip(tops, sums)]
        merged = [
            merge(blocks[i], h, part, jnp.where(counts[i] > 0, lse, NEG))
            for (i, h), (part, lse) in zip(chains, shares)
        ]
        for (i, h), (part, lse) in zip(chains, merged):
            finish(blocks[i], h, part, lse)

    def nothing(g):
        for i in range(GROUP):
            qb = plan[ORDER_AT + stage * ORDER + g * GROUP + i]
            for h in range(HEADS):
                finish(
                    qb, h, jnp.zeros((BLK, DH), jnp.bfloat16), jnp.full((BLK, DH), NEG, jnp.float32)
                )

    def any_group(g, carry):
        most = (plan[stage * COUNT + plan[ORDER_AT + stage * ORDER + g * GROUP]] + 1) >> 1
        if stage == 0:
            pl.when(most == 0)(functools.partial(nothing, g))
        for pairs in range(1, 5):
            pl.when(most == pairs)(functools.partial(group, g, pairs))
        return carry

    lax.fori_loop(0, QBS // GROUP, any_group, 0)

    for g in range(2):

        @pl.when(plan[DENSE_AT + g] >= 0)
        def _(g=g):
            qb = plan[DENSE_AT + g]
            queries = [load_q(qb, h) for h in range(HEADS)]

            def score(p, tops):
                tiles = [
                    dot_t(queries[h], kv_s[p, 0, :, h * DH : (h + 1) * DH]) for h in range(HEADS)
                ]
                for h in range(HEADS):
                    wide[h, p] = tiles[h]
                parts = [
                    [tile[:, t * DH : (t + 1) * DH] for t in range(TOK // DH)] for tile in tiles
                ]
                return tuple(
                    functools.reduce(jnp.maximum, part, top) for part, top in zip(parts, tops)
                )

            low = jnp.full((BLK, DH), NEG, jnp.float32)
            tops = lax.fori_loop(0, slots, score, (low,) * HEADS)
            tops = [jnp.max(top, axis=1, keepdims=True) for top in tops]

            def gather(p, sums):
                done = []
                for h in range(HEADS):
                    weights = jnp.exp2((wide[h, p] - tops[h]) * SCALE2).astype(jnp.bfloat16)
                    values = kv_s[p, 1, :, h * DH : (h + 1) * DH]
                    values = jnp.concatenate([values, jnp.ones_like(values)], axis=1)
                    done.append(
                        sums[h] + jnp.dot(weights, values, preferred_element_type=jnp.float32)
                    )
                return tuple(done)

            none = jnp.zeros((BLK, 2 * DH), jnp.float32)
            sums = lax.fori_loop(0, slots, gather, (none,) * HEADS)
            for h in range(HEADS):
                finish(qb, h, *merge(qb, h, *share(tops[h], sums[h])))

    eye = lax.broadcasted_iota(jnp.int32, (DH, DH), 0) == lax.broadcasted_iota(
        jnp.int32, (DH, DH), 1
    )
    for s in range(NX if last else 0):
        for h in range(HEADS):
            lines = []
            for t in range(TOK // DH):
                tile = stat[h, s * TOK + t * DH : s * TOK + (t + 1) * DH, :]
                lines.append(jnp.sum(jnp.where(eye, tile, 0.0), axis=0, keepdims=True))
            left = jnp.concatenate(lines, axis=0)
            terms = []
            for _ in range(3):
                term = left.astype(jnp.bfloat16).astype(jnp.float32)
                terms.append(term)
                left = left - term
            terms.append(jnp.zeros_like(left))
            o_s[s, TOK : TOK + STAT, h * DH : (h + 1) * DH] = jnp.concatenate(
                terms, axis=0
            ).astype(jnp.bfloat16)
    back = [pltpu.make_async_copy(a, b, sems.at[n]) for n, (a, b) in enumerate(out)]
    for copy in back:
        copy.start()
    for copy in back:
        copy.wait()


def attend(stage, plan, queries, pieces, before=()):
    slots = len(STAGES[stage])
    arrays = [*queries, *pieces, *before]
    rows = TOK + STAT
    held = [
        jax.ShapeDtypeStruct((NX, rows, ALL), jnp.bfloat16),
        jax.ShapeDtypeStruct((HEADS, NX * TOK, DH), jnp.float32),
    ]
    message = jax.ShapeDtypeStruct((rows, WIDE), jnp.bfloat16)
    last = stage == len(STAGES) - 1
    out_shape = [message] * (NX * HEADS // PAIR) if last else held
    return pl.pallas_call(
        functools.partial(attend_kernel, stage),
        out_shape=out_shape,
        in_specs=[in_smem] + [any_space] * len(arrays),
        out_specs=[any_space] * len(out_shape),
        scratch_shapes=[
            pltpu.VMEM((NX, rows, ALL), jnp.bfloat16),
            pltpu.VMEM((HEADS, NX * TOK, DH), jnp.float32),
            pltpu.VMEM((NX, TOK, ALL), jnp.bfloat16),
            pltpu.VMEM((slots, 2, TOK, ALL), jnp.bfloat16),
            pltpu.VMEM((HEADS, slots, BLK, TOK), jnp.float32),
            pltpu.SemaphoreType.DMA((24,)),
        ],
        compiler_params=pltpu.CompilerParams(vmem_limit_bytes=VMEM),
        cost_estimate=pl.CostEstimate(
            flops=8_000_000_000, bytes_accessed=24_000_000, transcendentals=4_000_000
        ),
    )(plan, *arrays)


def join_kernel(*refs):
    shares, out = refs[:-1], refs[-1]
    eye = lax.broadcasted_iota(jnp.int32, (DH, DH), 0) == lax.broadcasted_iota(
        jnp.int32, (DH, DH), 1
    )
    for h in range(PAIR):
        cols = slice(h * DH, (h + 1) * DH)
        stats = []
        for share in shares:
            terms = share[TOK : TOK + STAT, cols].astype(jnp.float32)
            stats.append(terms[0:4] + terms[4:8] + terms[8:12])
        for t in range(TOK // DH):
            lse = [
                jnp.sum(
                    jnp.where(eye, jnp.broadcast_to(s[t : t + 1], (DH, DH)), 0.0),
                    axis=1,
                    keepdims=True,
                )
                for s in stats
            ]
            top = functools.reduce(jnp.maximum, lse)
            scale = [jnp.exp(v - top) for v in lse]
            norm = functools.reduce(jnp.add, scale)
            rows = slice(t * DH, (t + 1) * DH)
            terms = [f * s[rows, cols].astype(jnp.float32) for f, s in zip(scale, shares)]
            out[rows, cols] = (functools.reduce(jnp.add, terms) / norm).astype(jnp.bfloat16)


def join(messages):
    return pl.pallas_call(
        join_kernel,
        out_shape=jax.ShapeDtypeStruct((TOK, WIDE), jnp.bfloat16),
        in_specs=[in_vmem] * len(messages),
        out_specs=in_vmem,
        compiler_params=pltpu.CompilerParams(vmem_limit_bytes=VMEM),
        cost_estimate=pl.CostEstimate(
            flops=4_000_000, bytes_accessed=1_300_000, transcendentals=8_000
        ),
    )(*messages)


def project_kernel(last, *refs):
    att, weight = refs[:NY], refs[NY : 2 * NY]
    total = functools.reduce(
        jnp.add,
        [jnp.dot(a[...], w[...], preferred_element_type=jnp.float32) for a, w in zip(att, weight)],
    )
    if last:
        total = total + refs[2 * NY][...]
    refs[-1][...] = total.astype(refs[-1].dtype)


def project(chunk, att, weight, so_far=None):
    last = so_far is not None
    columns = weight[0].shape[1]
    tile = 256
    out_spec = pl.BlockSpec((TOK, tile), lambda j: (0, j))
    return pl.pallas_call(
        functools.partial(project_kernel, last),
        grid=(columns // tile,),
        out_shape=jax.ShapeDtypeStruct((TOK, columns), jnp.bfloat16 if last else jnp.float32),
        in_specs=[pl.BlockSpec((TOK, WIDE), lambda j: (0, 0))] * NY
        + [pl.BlockSpec((WIDE, tile), lambda j: (chunk, j))] * NY
        + [out_spec] * last,
        out_specs=out_spec,
        compiler_params=pltpu.CompilerParams(vmem_limit_bytes=VMEM),
        cost_estimate=pl.CostEstimate(
            flops=1_073_741_824, bytes_accessed=5_000_000, transcendentals=0
        ),
    )(*att, *weight, *([so_far] if last else []))


def ring_step(right, left):
    return (
        lax.ppermute(right, "z", shift(NZ, 1)),
        lax.ppermute(left, "z", shift(NZ, -1)),
    )


def after(value, *others):
    return lax.optimization_barrier((value, others))[0]


def body(queries, key_value, out_weight, random_blocks, global_ids):
    z, x, y = lax.axis_index("z"), lax.axis_index("x"), lax.axis_index("head")
    own = jnp.transpose(key_value, (1, 0, 2))
    place = jnp.stack([z, x]).astype(jnp.int32)
    plane = (lax.all_gather(queries, "x"), queries)
    first = ring_step(own, own)
    plan = make_plan(random_blocks.reshape(-1), global_ids, place)
    columns = out_weight.shape[1] // NY
    weight = [
        lax.dynamic_slice_in_dim(out_weight, ((y + s) % NY) * columns, columns, axis=1)
        for s in range(NY)
    ]
    w1, w3 = (lax.ppermute(weight[s], "head", shift(NY, s)) for s in (1, 3))
    second = ring_step(*after(first, plan, weight))
    w2 = lax.ppermute(after(weight[2], w1, w3), "head", shift(NY, 2))
    third = ring_step(*after(second, w1, w3))
    near = [own, first[1], second[1], second[0], first[0]]
    held = attend(0, plan, plane, near)
    third = after(third, held, w2)
    fourth = ring_step(third[0][0], third[1][1])
    messages = attend(1, plan, plane, [third[1], *fourth, third[0]], held)
    weight = [weight[0], w1, w2, w3]
    total = None
    for c in range(HEADS // PAIR):
        sent = messages[c * NX : (c + 1) * NX]
        shares = [sent[0]] + [lax.ppermute(sent[s], "x", shift(NX, -s)) for s in range(1, NX)]
        att = join(shares)
        everyone = [att] + [lax.ppermute(att, "head", shift(NY, s)) for s in range(1, NY)]
        total = project(c, everyone, weight, total)
    return total


def solution(mesh):
    devices = mesh.devices.reshape(mesh.devices.shape[0], NZ, NX, NY)
    grid = Mesh(devices, ("batch", "z", "x", "head"))
    rows = ("batch", "z", "x")
    in_specs = (
        P(rows, "head"),
        P(rows, None, "head"),
        P("head", None),
        P("batch", None),
        P("batch"),
    )
    return jax.shard_map(
        body, mesh=grid, in_specs=in_specs, out_specs=P(rows, "head"), check_vma=False
    )
```

time: 226 us -> 171 us (0.76)
  the two profiles are of different devices: /device:TPU:103 before, /device:TPU:72 now
where the time goes in v2:
time: 171 us; the launch traced here: 168 us
  waiting for transfers between devices  73 us (43%)
  starting transfers between devices  38.5 us (23%)
  Pallas kernels  30.9 us (18%)
  between operations  13.5 us (8%)
  local copies, waits for them, and re-layouts  11.6 us (7%)
    ppermute x4, waiting for transfers between devices, ring_step(): lax.ppermute(right, 'z', shift(NZ, 1))  38.1 us
    ppermute x6, starting transfers between devices, body(): lax.ppermute(sent[s], 'x', shift(NX, -s))  14.9 us
    pallas_call x2, Pallas kernels, attend(): pl.pallas_call(functools.partial(attend_kernel, stage), out_shape=out_sha...  14.7 us
    ppermute x4, waiting for transfers between devices, ring_step(): lax.ppermute(left, 'z', shift(NZ, -1))  14.4 us
    ppermute x6, waiting for transfers between devices, body(): lax.ppermute(sent[s], 'x', shift(NX, -s))  11.1 us
    ppermute x6, starting transfers between devices, body(): lax.ppermute(att, 'head', shift(NY, s))  10 us
    ppermute x4, starting transfers between devices, ring_step(): lax.ppermute(right, 'z', shift(NZ, 1))  8.69 us
    ppermute x6, waiting for transfers between devices, body(): lax.ppermute(att, 'head', shift(NY, s))  7.78 us
  transfers between devices with their start and end apart: 24, of which 16 were waited for; matrix products, arithmetic and copies ran while one was open for 5% of the time, Pallas kernels for 13%

profile of v2, /device:TPU:72, one launch (start us, length us, event | category | flops | bytes accessed | tf_op | source)
XLA Modules:
  0.0 167.7 jit_solution(11461790953960530540)
XLA Ops:
  7.3 2.4 %copy.11 = bf16[512,2,512]{2,0,1:T(8,128)(2,1)} copy(bf16[512,2,512]{2,1,0:T(2,128)(2,1)} %param.7) | data formatting | bytes 2097152 | tf_op args[1]
  9.6 1.9 %collective-permute-start = (bf16[2,512,512]{2,1,0:T(8,128)(2,1)}, bf16[2,512,512]{2,1,0:T(8,128)(2,1)}, u32[]{:S(2)}, u32[]{:S(2)}) collective-permute-start(bf16[2,512,512]{2,1,0:T(8,128)(2,1)} %bitcast.9.refs_3_), channel_id=1, source_target_pairs={{0,16},{16,32},{32,48},{48,64},{64,80},{80,96},{96,112},{112,0},{1... | collective-permute-start | bytes 3145736 | tf_op jit(solution)/shard_map/ppermute | solution.py:420
  11.7 4.1 %constant_dynamic-slice_fusion = (bf16[512,1024]{1,0:T(8,128)(2,1)}, bf16[512,1024]{1,0:T(8,128)(2,1)}, bf16[512,1024]{1,0:T(8,128)(2,1)S(1)}, bf16[512,1024]{1,0:T(8,128)(2,1)}) fusion(bf16[512,4096]{1,0:T(8,128)(2,1)} %param.8, s32[]{:T(128)S(6)} %select_n.38, s32[]{:T(128)S(6)} %select_n.34, s32[]{:T(128)S(6)} %select_n.32, s32[]{:T(128)S(6)} %select_n.36), kind=kLoop, calls=%fused_computation.3 | loop fusion | bytes 8388624 | tf_op jit(solution)/shard_map/dynamic_slice | solution.py:438
  15.8 1.6 collective-permute-start.4
  18.3 6.9 %shard_map.64.refs_0_ = s32[675]{0:T(1024)S(1)} custom-call(s32[768]{0:T(1024)S(1)} %reshape.3.table, s32[2]{0:T(128)S(1)} %copy-done.1, s32[2]{0:T(128)S(1)} %pad_add_fusion.place, s32[8]{0:T(128)S(1)} %copy-done.2), custom_call_target="tpu_custom_call" | custom-call | tf_op jit(solution)/shard_map/pallas_call | solution.py:102
  25.2 9.6 %collective-permute-done.refs_7_ = bf16[2,512,512]{2,1,0:T(8,128)(2,1)} collective-permute-done((bf16[2,512,512]{2,1,0:T(8,128)(2,1)}, bf16[2,512,512]{2,1,0:T(8,128)(2,1)}, u32[]{:S(2)}, u32[]{:S(2)}) %collective-permute-start) | collective-permute-done | bytes 1048608 | tf_op jit(solution)/shard_map/ppermute | solution.py:420
  34.8 3.1 %collective-permute-done.1.refs_4_ = bf16[2,512,512]{2,1,0:T(8,128)(2,1)} collective-permute-done((bf16[2,512,512]{2,1,0:T(8,128)(2,1)}, bf16[2,512,512]{2,1,0:T(8,128)(2,1)}, u32[]{:S(2)}, u32[]{:S(2)}) %collective-permute-start.1) | collective-permute-done | bytes 1048608 | tf_op jit(solution)/shard_map/ppermute | solution.py:421
  37.9 2.9 %collective-permute-start.2 = (bf16[2,512,512]{2,1,0:T(8,128)(2,1)}, bf16[2,512,512]{2,1,0:T(8,128)(2,1)}, u32[]{:S(2)}, u32[]{:S(2)}) collective-permute-start(bf16[2,512,512]{2,1,0:T(8,128)(2,1)} %collective-permute-done.refs_7_), channel_id=1, source_target_pairs={{0,16},{16,32},{32,48},{48,64},{64,80},{80,96},{96,112},{112,0},{1... | collective-permute-start | bytes 3145736 | tf_op jit(solution)/shard_map/ppermute | solution.py:420
  41.8 2.2 %collective-permute-start.8 = (bf16[512,1024]{1,0:T(8,128)(2,1)}, bf16[512,1024]{1,0:T(8,128)(2,1)}, u32[]{:S(2)}, u32[]{:S(2)}) collective-permute-start(bf16[512,1024]{1,0:T(8,128)(2,1)} %get-tuple-element.28), channel_id=1, source_target_pairs={{0,2},{1,3},{2,0},{3,1},{4,6},{5,7},{6,4},{7,5},{8,10},{9,11},{10,... | collective-permute-start | bytes 3145736 | tf_op jit(solution)/shard_map/ppermute | solution.py:443
  44.0 18.3 %collective-permute-done.2.refs_6_ = bf16[2,512,512]{2,1,0:T(8,128)(2,1)} collective-permute-done((bf16[2,512,512]{2,1,0:T(8,128)(2,1)}, bf16[2,512,512]{2,1,0:T(8,128)(2,1)}, u32[]{:S(2)}, u32[]{:S(2)}) %collective-permute-start.2) | collective-permute-done | bytes 1048608 | tf_op jit(solution)/shard_map/ppermute | solution.py:420
  62.4 2.2 %collective-permute-done.3.refs_5_ = bf16[2,512,512]{2,1,0:T(8,128)(2,1)} collective-permute-done((bf16[2,512,512]{2,1,0:T(8,128)(2,1)}, bf16[2,512,512]{2,1,0:T(8,128)(2,1)}, u32[]{:S(2)}, u32[]{:S(2)}) %collective-permute-start.3) | collective-permute-done | bytes 1048608 | tf_op jit(solution)/shard_map/ppermute | solution.py:421
  64.6 1.8 %collective-permute-start.6 = (bf16[2,512,512]{2,1,0:T(8,128)(2,1)}, bf16[2,512,512]{2,1,0:T(8,128)(2,1)}, u32[]{:S(2)}, u32[]{:S(2)}) collective-permute-start(bf16[2,512,512]{2,1,0:T(8,128)(2,1)} %collective-permute-done.2.refs_6_), channel_id=1, source_target_pairs={{0,16},{16,32},{32,48},{48,64},{64,80},{80,96},{96,112},{112,0},{1... | collective-permute-start | bytes 3145736 | tf_op jit(solution)/shard_map/ppermute | solution.py:420
  67.6 1.6 copy-done.3
  69.2 9.2 %shard_map.65 = (bf16[4,528,512]{2,1,0:T(8,128)(2,1)S(1)}, f32[4,2048,128]{2,1,0:T(8,128)S(1)}) custom-call(s32[675]{0:T(1024)S(1)} %shard_map.64.refs_0_, bf16[4,512,512]{2,1,0:T(8,128)(2,1)S(1)} %bitcast.10, bf16[512,512]{1,0:T(8,128)(2,1)S(1)} %copy-done, bf16[2,512,512]{2,1,0:T(8,128)(2,1)} %bitcast.9.refs_3_, ...), custom_call_target="tpu_custom_call" | custom-call | flops 8000000000 | bytes 24000000 | tf_op jit(solution)/shard_map/pallas_call | solution.py:326
  78.4 9.0 %collective-permute-done.6.refs_6_ = bf16[2,512,512]{2,1,0:T(8,128)(2,1)} collective-permute-done((bf16[2,512,512]{2,1,0:T(8,128)(2,1)}, bf16[2,512,512]{2,1,0:T(8,128)(2,1)}, u32[]{:S(2)}, u32[]{:S(2)}) %collective-permute-start.6) | collective-permute-done | bytes 1048608 | tf_op jit(solution)/shard_map/ppermute | solution.py:420
  87.4 1.9 %collective-permute-done.7.refs_3_ = bf16[2,512,512]{2,1,0:T(8,128)(2,1)} collective-permute-done((bf16[2,512,512]{2,1,0:T(8,128)(2,1)}, bf16[2,512,512]{2,1,0:T(8,128)(2,1)}, u32[]{:S(2)}, u32[]{:S(2)}) %collective-permute-start.7) | collective-permute-done | bytes 1048608 | tf_op jit(solution)/shard_map/ppermute | solution.py:421
  91.7 2.0 %collective-permute-start.9 = (bf16[512,512]{1,0:T(8,128)(2,1)S(1)}, bf16[512,512]{1,0:T(8,128)(2,1)S(1)}, u32[]{:S(2)}, u32[]{:S(2)}) collective-permute-start(bf16[512,512]{1,0:T(8,128)(2,1)S(1)} %slice_bitcast_fusion.1), channel_id=1, source_target_pairs={{0,16},{16,32},{32,48},{48,64},{64,80},{80,96},{96,112},{112,0},{1... | collective-permute-start | bytes 1572872 | tf_op jit(solution)/shard_map/ppermute | solution.py:420
  93.8 7.3 %collective-permute-done.10.refs_5_ = bf16[512,512]{1,0:T(8,128)(2,1)S(1)} collective-permute-done((bf16[512,512]{1,0:T(8,128)(2,1)S(1)}, bf16[512,512]{1,0:T(8,128)(2,1)S(1)}, u32[]{:S(2)}, u32[]{:S(2)}) %collective-permute-start.10) | collective-permute-done | bytes 524320 | tf_op jit(solution)/shard_map/ppermute | solution.py:421
  102.2 5.6 %shard_map.66 = (bf16[528,256]{1,0:T(8,128)(2,1)S(1)}, bf16[528,256]{1,0:T(8,128)(2,1)S(1)}, bf16[528,256]{1,0:T(8,128)(2,1)S(1)}, bf16[528,256]{1,0:T(8,128)(2,...) custom-call(s32[675]{0:T(1024)S(1)} %shard_map.64.refs_0_, ...), custom_call_target="tpu_custom_call" | custom-call | flops 8000000000 | bytes 24000000 | tf_op jit(solution)/shard_map/pallas_call | solution.py:326
  107.8 9.3 %collective-permute-start.17 = (bf16[528,256]{1,0:T(8,128)(2,1)S(1)}, bf16[528,256]{1,0:T(8,128)(2,1)S(1)}, u32[]{:S(2)}, u32[]{:S(2)}) collective-permute-start(bf16[528,256]{1,0:T(8,128)(2,1)S(1)} %get-tuple-element.36), channel_id=1, source_target_pairs={{0,12},{4,0},{8,4},{12,8},{1,13},{5,1},{9,5},{13,9},{2,14},{6,2},{... | collective-permute-start | bytes 811016 | tf_op jit(solution)/shard_map/ppermute | solution.py:454
  118.1 2.3 %collective-permute-start.11 = (bf16[528,256]{1,0:T(8,128)(2,1)S(1)}, bf16[528,256]{1,0:T(8,128)(2,1)S(1)}, u32[]{:S(2)}, u32[]{:S(2)}) collective-permute-start(bf16[528,256]{1,0:T(8,128)(2,1)S(1)} %get-tuple-element.32), channel_id=1, source_target_pairs={{0,12},{4,0},{8,4},{12,8},{1,13},{5,1},{9,5},{13,9},{2,14},{6,2},{... | collective-permute-start | bytes 811016 | tf_op jit(solution)/shard_map/ppermute | solution.py:454
  120.3 2.3 %collective-permute-start.12 = (bf16[528,256]{1,0:T(8,128)(2,1)S(1)}, bf16[528,256]{1,0:T(8,128)(2,1)S(1)}, u32[]{:S(2)}, u32[]{:S(2)}) collective-permute-start(bf16[528,256]{1,0:T(8,128)(2,1)S(1)} %get-tuple-element.33), channel_id=1, source_target_pairs={{0,8},{4,12},{8,0},{12,4},{1,9},{5,13},{9,1},{13,5},{2,10},{6,14},... | collective-permute-start | bytes 811016 | tf_op jit(solution)/shard_map/ppermute | solution.py:454
  122.7 6.0 %collective-permute-done.17.refs_1_ = bf16[528,256]{1,0:T(8,128)(2,1)S(1)} collective-permute-done((bf16[528,256]{1,0:T(8,128)(2,1)S(1)}, bf16[528,256]{1,0:T(8,128)(2,1)S(1)}, u32[]{:S(2)}, u32[]{:S(2)}) %collective-permute-start.17) | collective-permute-done | bytes 270368 | tf_op jit(solution)/shard_map/ppermute | solution.py:454
  128.7 4.8 %collective-permute-done.19.refs_3_ = bf16[528,256]{1,0:T(8,128)(2,1)S(1)} collective-permute-done((bf16[528,256]{1,0:T(8,128)(2,1)S(1)}, bf16[528,256]{1,0:T(8,128)(2,1)S(1)}, u32[]{:S(2)}, u32[]{:S(2)}) %collective-permute-start.19) | collective-permute-done | bytes 270368 | tf_op jit(solution)/shard_map/ppermute | solution.py:454
  134.3 1.7 collective-permute-start.20
  136.9 2.4 %collective-permute-start.22 = (bf16[512,256]{1,0:T(8,128)(2,1)S(1)}, bf16[512,256]{1,0:T(8,128)(2,1)S(1)}, u32[]{:S(2)}, u32[]{:S(2)}) collective-permute-start(bf16[512,256]{1,0:T(8,128)(2,1)S(1)} %shard_map.68.refs_0_), channel_id=1, source_target_pairs={{0,3},{1,0},{2,1},{3,2},{4,7},{5,4},{6,5},{7,6},{8,11},{9,8},{10,9... | collective-permute-start | bytes 786440 | tf_op jit(solution)/shard_map/ppermute | solution.py:456
  140.4 1.7 collective-permute-start.14
  143.6 1.8 %collective-permute-start.16 = (bf16[512,256]{1,0:T(8,128)(2,1)S(1)}, bf16[512,256]{1,0:T(8,128)(2,1)S(1)}, u32[]{:S(2)}, u32[]{:S(2)}) collective-permute-start(bf16[512,256]{1,0:T(8,128)(2,1)S(1)} %shard_map.67.refs_0_), channel_id=1, source_target_pairs={{0,3},{1,0},{2,1},{3,2},{4,7},{5,4},{6,5},{7,6},{8,11},{9,8},{10,9... | collective-permute-start | bytes 786440 | tf_op jit(solution)/shard_map/ppermute | solution.py:456
  146.7 3.7 %collective-permute-done.22.refs_3_ = bf16[512,256]{1,0:T(8,128)(2,1)S(1)} collective-permute-done((bf16[512,256]{1,0:T(8,128)(2,1)S(1)}, bf16[512,256]{1,0:T(8,128)(2,1)S(1)}, u32[]{:S(2)}, u32[]{:S(2)}) %collective-permute-start.22) | collective-permute-done | bytes 262176 | tf_op jit(solution)/shard_map/ppermute | solution.py:456
  150.3 3.4 %shard_map.69.refs_8_ = f32[512,1024]{1,0:T(8,128)S(1)} custom-call(bf16[512,256]{1,0:T(8,128)(2,1)S(1)} %shard_map.68.refs_0_, bf16[512,256]{1,0:T(8,128)(2,1)S(1)} %collective-permute-done.20.refs_1_, bf16[512,256]{1,0:T(8,128)(2,1)S(1)} %collective-permute-done.21.refs_2_, bf16[512,256]{1,0:T(8,128)(2,1)S(1)} %collective-permute-done.22.refs_3_, ...), custom_call_target="tpu_custom_call" | custom-call | flops 1073741824 | bytes 5000000 | tf_op jit(solution)/shard_map/pallas_call | solution.py:403
  154.0 2.7 %collective-permute-done.16.refs_3_ = bf16[512,256]{1,0:T(8,128)(2,1)S(1)} collective-permute-done((bf16[512,256]{1,0:T(8,128)(2,1)S(1)}, bf16[512,256]{1,0:T(8,128)(2,1)S(1)}, u32[]{:S(2)}, u32[]{:S(2)}) %collective-permute-start.16) | collective-permute-done | bytes 262176 | tf_op jit(solution)/shard_map/ppermute | solution.py:456
  156.7 4.2 %shard_map.70 = bf16[512,1024]{1,0:T(8,128)(2,1)} custom-call(bf16[512,256]{1,0:T(8,128)(2,1)S(1)} %shard_map.67.refs_0_, bf16[512,256]{1,0:T(8,128)(2,1)S(1)} %collective-permute-done.14.refs_1_, bf16[512,256]{1,0:T(8,128)(2,1)S(1)} %collective-permute-done.15.refs_2_, bf16[512,256]{1,0:T(8,128)(2,1)S(1)} %collective-permute-done.16.refs_3_, ...), custom_call_target="tpu_custom_call" | custom-call | flops 1073741824 | bytes 5000000 | tf_op jit(solution)/shard_map/pallas_call | solution.py:403
  (41 shorter events, 14.5 us)
Async XLA Ops:
  6.5 60.0 %all-gather.3.cloned.1.call-start = ((), (), s32[]{:S(2)}) async-start(), calls=%async_computation | async-start | bytes 2621440 | tf_op jit(solution)/shard_map/all_gather | solution.py:433
  9.6 25.2 %collective-permute-start = (bf16[2,512,512]{2,1,0:T(8,128)(2,1)}, bf16[2,512,512]{2,1,0:T(8,128)(2,1)}, u32[]{:S(2)}, u32[]{:S(2)}) collective-permute-start(bf16[2,512,512]{2,1,0:T(8,128)(2,1)} %bitcast.9.refs_3_), channel_id=1, source_target_pairs={{0,16},{16,32},{32,48},{48,64},{64,80},{80,96},{96,112},{112,0},{1... | collective-permute-start | bytes 3145736 | tf_op jit(solution)/shard_map/ppermute | solution.py:420
  11.5 26.4 %collective-permute-start.1 = (bf16[2,512,512]{2,1,0:T(8,128)(2,1)}, bf16[2,512,512]{2,1,0:T(8,128)(2,1)}, u32[]{:S(2)}, u32[]{:S(2)}) collective-permute-start(bf16[2,512,512]{2,1,0:T(8,128)(2,1)} %bitcast.9.refs_3_), channel_id=1, source_target_pairs={{0,112},{16,0},{32,16},{48,32},{64,48},{80,64},{96,80},{112,96},{1... | collective-permute-start | bytes 3145736 | tf_op jit(solution)/shard_map/ppermute | solution.py:421
  11.6 6.2 %copy-start.4 = (s32[256,3]{0,1:T(4,128)S(1)}, s32[256,3]{0,1:T(4,128)}, u32[]{:S(2)}) copy-start(s32[256,3]{0,1:T(4,128)} %param.9) | copy-start | bytes 9220
  11.6 6.6 %copy-start.1 = (s32[2]{0:T(128)S(1)}, s32[2]{0:T(128)}, u32[]{:S(2)}) copy-start(s32[2]{0:T(128)} %glob.1) | copy-start | bytes 28
  11.6 6.6 %copy-start.2 = (s32[8]{0:T(128)S(1)}, s32[8]{0:T(128)}, u32[]{:S(2)}) copy-start(s32[8]{0:T(128)} %constant.50.clone.slots) | copy-start | bytes 100
  15.8 25.0 %collective-permute-start.4 = (bf16[512,1024]{1,0:T(8,128)(2,1)}, bf16[512,1024]{1,0:T(8,128)(2,1)S(1)}, u32[]{:S(2)}, u32[]{:S(2)}) collective-permute-start(bf16[512,1024]{1,0:T(8,128)(2,1)} %get-tuple-element.40), channel_id=1, source_target_pairs={{0,1},{1,2},{2,3},{3,0},{4,5},{5,6},{6,7},{7,4},{8,9},{9,10},{10,1... | collective-permute-start | bytes 3145736 | tf_op jit(solution)/shard_map/ppermute | solution.py:441
  17.4 24.4 %collective-permute-start.5 = (bf16[512,1024]{1,0:T(8,128)(2,1)}, bf16[512,1024]{1,0:T(8,128)(2,1)S(1)}, u32[]{:S(2)}, u32[]{:S(2)}) collective-permute-start(bf16[512,1024]{1,0:T(8,128)(2,1)} %get-tuple-element.39), channel_id=1, source_target_pairs={{0,3},{1,0},{2,1},{3,2},{4,7},{5,4},{6,5},{7,6},{8,11},{9,8},{10,9... | collective-permute-start | bytes 3145736 | tf_op jit(solution)/shard_map/ppermute | solution.py:441
  37.9 24.5 %collective-permute-start.2 = (bf16[2,512,512]{2,1,0:T(8,128)(2,1)}, bf16[2,512,512]{2,1,0:T(8,128)(2,1)}, u32[]{:S(2)}, u32[]{:S(2)}) collective-permute-start(bf16[2,512,512]{2,1,0:T(8,128)(2,1)} %collective-permute-done.refs_7_), channel_id=1, source_target_pairs={{0,16},{16,32},{32,48},{48,64},{64,80},{80,96},{96,112},{112,0},{1... | collective-permute-start | bytes 3145736 | tf_op jit(solution)/shard_map/ppermute | solution.py:420
  40.8 23.7 %collective-permute-start.3 = (bf16[2,512,512]{2,1,0:T(8,128)(2,1)}, bf16[2,512,512]{2,1,0:T(8,128)(2,1)}, u32[]{:S(2)}, u32[]{:S(2)}) collective-permute-start(bf16[2,512,512]{2,1,0:T(8,128)(2,1)} %collective-permute-done.1.refs_4_), channel_id=1, source_target_pairs={{0,112},{16,0},{32,16},{48,32},{64,48},{80,64},{96,80},{112,96},{1... | collective-permute-start | bytes 3145736 | tf_op jit(solution)/shard_map/ppermute | solution.py:421
  41.8 36.6 %collective-permute-start.8 = (bf16[512,1024]{1,0:T(8,128)(2,1)}, bf16[512,1024]{1,0:T(8,128)(2,1)}, u32[]{:S(2)}, u32[]{:S(2)}) collective-permute-start(bf16[512,1024]{1,0:T(8,128)(2,1)} %get-tuple-element.28), channel_id=1, source_target_pairs={{0,2},{1,3},{2,0},{3,1},{4,6},{5,7},{6,4},{7,5},{8,10},{9,11},{10,... | collective-permute-start | bytes 3145736 | tf_op jit(solution)/shard_map/ppermute | solution.py:443
  64.6 22.8 %collective-permute-start.6 = (bf16[2,512,512]{2,1,0:T(8,128)(2,1)}, bf16[2,512,512]{2,1,0:T(8,128)(2,1)}, u32[]{:S(2)}, u32[]{:S(2)}) collective-permute-start(bf16[2,512,512]{2,1,0:T(8,128)(2,1)} %collective-permute-done.2.refs_6_), channel_id=1, source_target_pairs={{0,16},{16,32},{32,48},{48,64},{64,80},{80,96},{96,112},{112,0},{1... | collective-permute-start | bytes 3145736 | tf_op jit(solution)/shard_map/ppermute | solution.py:420
  66.4 22.9 %collective-permute-start.7 = (bf16[2,512,512]{2,1,0:T(8,128)(2,1)}, bf16[2,512,512]{2,1,0:T(8,128)(2,1)}, u32[]{:S(2)}, u32[]{:S(2)}) collective-permute-start(bf16[2,512,512]{2,1,0:T(8,128)(2,1)} %collective-permute-done.3.refs_5_), channel_id=1, source_target_pairs={{0,112},{16,0},{32,16},{48,32},{64,48},{80,64},{96,80},{112,96},{1... | collective-permute-start | bytes 3145736 | tf_op jit(solution)/shard_map/ppermute | solution.py:421
  66.6 1.0 copy-start
  67.6 1.6 copy-start.3
  90.3 10.8 %collective-permute-start.10 = (bf16[512,512]{1,0:T(8,128)(2,1)S(1)}, bf16[512,512]{1,0:T(8,128)(2,1)S(1)}, u32[]{:S(2)}, u32[]{:S(2)}) collective-permute-start(bf16[512,512]{1,0:T(8,128)(2,1)S(1)} %slice_bitcast_fusion), channel_id=1, source_target_pairs={{0,112},{16,0},{32,16},{48,32},{64,48},{80,64},{96,80},{112,96},{1... | collective-permute-start | bytes 1572872 | tf_op jit(solution)/shard_map/ppermute | solution.py:421
  91.7 10.5 %collective-permute-start.9 = (bf16[512,512]{1,0:T(8,128)(2,1)S(1)}, bf16[512,512]{1,0:T(8,128)(2,1)S(1)}, u32[]{:S(2)}, u32[]{:S(2)}) collective-permute-start(bf16[512,512]{1,0:T(8,128)(2,1)S(1)} %slice_bitcast_fusion.1), channel_id=1, source_target_pairs={{0,16},{16,32},{32,48},{48,64},{64,80},{80,96},{96,112},{112,0},{1... | collective-permute-start | bytes 1572872 | tf_op jit(solution)/shard_map/ppermute | solution.py:420
  107.8 20.9 %collective-permute-start.17 = (bf16[528,256]{1,0:T(8,128)(2,1)S(1)}, bf16[528,256]{1,0:T(8,128)(2,1)S(1)}, u32[]{:S(2)}, u32[]{:S(2)}) collective-permute-start(bf16[528,256]{1,0:T(8,128)(2,1)S(1)} %get-tuple-element.36), channel_id=1, source_target_pairs={{0,12},{4,0},{8,4},{12,8},{1,13},{5,1},{9,5},{13,9},{2,14},{6,2},{... | collective-permute-start | bytes 811016 | tf_op jit(solution)/shard_map/ppermute | solution.py:454
  117.1 11.6 %collective-permute-start.18 = (bf16[528,256]{1,0:T(8,128)(2,1)S(1)}, bf16[528,256]{1,0:T(8,128)(2,1)S(1)}, u32[]{:S(2)}, u32[]{:S(2)}) collective-permute-start(bf16[528,256]{1,0:T(8,128)(2,1)S(1)} %get-tuple-element.37), channel_id=1, source_target_pairs={{0,8},{4,12},{8,0},{12,4},{1,9},{5,13},{9,1},{13,5},{2,10},{6,14},... | collective-permute-start | bytes 811016 | tf_op jit(solution)/shard_map/ppermute | solution.py:454
  117.1 16.3 %collective-permute-start.19 = (bf16[528,256]{1,0:T(8,128)(2,1)S(1)}, bf16[528,256]{1,0:T(8,128)(2,1)S(1)}, u32[]{:S(2)}, u32[]{:S(2)}) collective-permute-start(bf16[528,256]{1,0:T(8,128)(2,1)S(1)} %get-tuple-element.38), channel_id=1, source_target_pairs={{0,4},{4,8},{8,12},{12,0},{1,5},{5,9},{9,13},{13,1},{2,6},{6,10},{... | collective-permute-start | bytes 811016 | tf_op jit(solution)/shard_map/ppermute | solution.py:454
  118.1 18.8 %collective-permute-start.11 = (bf16[528,256]{1,0:T(8,128)(2,1)S(1)}, bf16[528,256]{1,0:T(8,128)(2,1)S(1)}, u32[]{:S(2)}, u32[]{:S(2)}) collective-permute-start(bf16[528,256]{1,0:T(8,128)(2,1)S(1)} %get-tuple-element.32), channel_id=1, source_target_pairs={{0,12},{4,0},{8,4},{12,8},{1,13},{5,1},{9,5},{13,9},{2,14},{6,2},{... | collective-permute-start | bytes 811016 | tf_op jit(solution)/shard_map/ppermute | solution.py:454
  120.3 19.0 %collective-permute-start.12 = (bf16[528,256]{1,0:T(8,128)(2,1)S(1)}, bf16[528,256]{1,0:T(8,128)(2,1)S(1)}, u32[]{:S(2)}, u32[]{:S(2)}) collective-permute-start(bf16[528,256]{1,0:T(8,128)(2,1)S(1)} %get-tuple-element.33), channel_id=1, source_target_pairs={{0,8},{4,12},{8,0},{12,4},{1,9},{5,13},{9,1},{13,5},{2,10},{6,14},... | collective-permute-start | bytes 811016 | tf_op jit(solution)/shard_map/ppermute | solution.py:454
  128.7 10.9 %collective-permute-start.13 = (bf16[528,256]{1,0:T(8,128)(2,1)S(1)}, bf16[528,256]{1,0:T(8,128)(2,1)S(1)}, u32[]{:S(2)}, u32[]{:S(2)}) collective-permute-start(bf16[528,256]{1,0:T(8,128)(2,1)S(1)} %get-tuple-element.34), channel_id=1, source_target_pairs={{0,4},{4,8},{8,12},{12,0},{1,5},{5,9},{9,13},{13,1},{2,6},{6,10},{... | collective-permute-start | bytes 811016 | tf_op jit(solution)/shard_map/ppermute | solution.py:454
  134.3 9.4 %collective-permute-start.20 = (bf16[512,256]{1,0:T(8,128)(2,1)S(1)}, bf16[512,256]{1,0:T(8,128)(2,1)S(1)}, u32[]{:S(2)}, u32[]{:S(2)}) collective-permute-start(bf16[512,256]{1,0:T(8,128)(2,1)S(1)} %shard_map.68.refs_0_), channel_id=1, source_target_pairs={{0,1},{1,2},{2,3},{3,0},{4,5},{5,6},{6,7},{7,4},{8,9},{9,10},{10,1... | collective-permute-start | bytes 786440 | tf_op jit(solution)/shard_map/ppermute | solution.py:456
  135.9 10.7 %collective-permute-start.21 = (bf16[512,256]{1,0:T(8,128)(2,1)S(1)}, bf16[512,256]{1,0:T(8,128)(2,1)S(1)}, u32[]{:S(2)}, u32[]{:S(2)}) collective-permute-start(bf16[512,256]{1,0:T(8,128)(2,1)S(1)} %shard_map.68.refs_0_), channel_id=1, source_target_pairs={{0,2},{1,3},{2,0},{3,1},{4,6},{5,7},{6,4},{7,5},{8,10},{9,11},{10,... | collective-permute-start | bytes 786440 | tf_op jit(solution)/shard_map/ppermute | solution.py:456
  136.9 13.4 %collective-permute-start.22 = (bf16[512,256]{1,0:T(8,128)(2,1)S(1)}, bf16[512,256]{1,0:T(8,128)(2,1)S(1)}, u32[]{:S(2)}, u32[]{:S(2)}) collective-permute-start(bf16[512,256]{1,0:T(8,128)(2,1)S(1)} %shard_map.68.refs_0_), channel_id=1, source_target_pairs={{0,3},{1,0},{2,1},{3,2},{4,7},{5,4},{6,5},{7,6},{8,11},{9,8},{10,9... | collective-permute-start | bytes 786440 | tf_op jit(solution)/shard_map/ppermute | solution.py:456
  140.4 13.3 %collective-permute-start.14 = (bf16[512,256]{1,0:T(8,128)(2,1)S(1)}, bf16[512,256]{1,0:T(8,128)(2,1)S(1)}, u32[]{:S(2)}, u32[]{:S(2)}) collective-permute-start(bf16[512,256]{1,0:T(8,128)(2,1)S(1)} %shard_map.67.refs_0_), channel_id=1, source_target_pairs={{0,1},{1,2},{2,3},{3,0},{4,5},{5,6},{6,7},{7,4},{8,9},{9,10},{10,1... | collective-permute-start | bytes 786440 | tf_op jit(solution)/shard_map/ppermute | solution.py:456
  142.1 11.9 %collective-permute-start.15 = (bf16[512,256]{1,0:T(8,128)(2,1)S(1)}, bf16[512,256]{1,0:T(8,128)(2,1)S(1)}, u32[]{:S(2)}, u32[]{:S(2)}) collective-permute-start(bf16[512,256]{1,0:T(8,128)(2,1)S(1)} %shard_map.67.refs_0_), channel_id=1, source_target_pairs={{0,2},{1,3},{2,0},{3,1},{4,6},{5,7},{6,4},{7,5},{8,10},{9,11},{10,... | collective-permute-start | bytes 786440 | tf_op jit(solution)/shard_map/ppermute | solution.py:456
  143.6 13.0 %collective-permute-start.16 = (bf16[512,256]{1,0:T(8,128)(2,1)S(1)}, bf16[512,256]{1,0:T(8,128)(2,1)S(1)}, u32[]{:S(2)}, u32[]{:S(2)}) collective-permute-start(bf16[512,256]{1,0:T(8,128)(2,1)S(1)} %shard_map.67.refs_0_), channel_id=1, source_target_pairs={{0,3},{1,0},{2,1},{3,2},{4,7},{5,4},{6,5},{7,6},{8,11},{9,8},{10,9... | collective-permute-start | bytes 786440 | tf_op jit(solution)/shard_map/ppermute | solution.py:456
Sparse Core Ops, SparseCore 0:
  9.2 35.5 all-gather.2
